TPU v7x, 256 devices: a whole 4x4x8 slice. The times are simulated.
256 devices in a mesh: pitch: 16 (over x_hi, z), inst: 8 (over y, core), span: 2 (over x_lo).
Axes of the slice: x: 4 (x_hi: 2, x_lo: 2; x = x_hi * 2 + x_lo), y: 4, z: 8, core: 2. Of those that a mesh axis runs over, the one named last changes fastest.
Arguments:
- donor_state: float32 [2, 24, 5, 128, 2048], P(None, 'inst', None, 'span', 'pitch'), may hold values from -6 to 6
- time_shift: float32 [2, 17, 17], replicated, may hold values from -1.5 to 1.5
- face_shift: int32 [17], replicated, may hold values from 0 to 1023, as said below
- weights: float32 [2, 4, 2048], P(None, None, 'pitch'), may hold values from 0.1 to 0.5
- offsets: int32 [2, 4], replicated, may hold values from -3 to 3
Outputs:
- received: float32 [2, 24, 5, 128, 2048], P(None, 'inst', None, 'span', 'pitch')
Inputs may be any that keep to these rules, and one draw needn't show every extreme that they name: `face_shift`: at least one instance has a shift of 960 or more.
All inputs are finite; a program needn't handle non-finite values.
Results may differ from a plain program's by a relative error of at most 0.00007.
Values sent between devices are 32-bit elements; how exact they have to be, the bound alone decides.
No kernel may reach another device: no remote copies, remote signals or barrier semaphores. Data moves between devices by JAX's collectives and lax.ppermute only.
A program may use at most 128 MiB of HBM per device.

v0:
```python
import jax
import jax.numpy as jnp
from jax import lax
from jax.sharding import PartitionSpec as P


def in_order(parts, dim):
    shape = list(parts.shape[1:])
    shape[dim] *= parts.shape[0]
    return jnp.moveaxis(parts, 0, dim).reshape(shape)


def sent_to_all(x, axis):
    count = lax.axis_size(axis)
    return lax.all_to_all(jnp.broadcast_to(x[None], (count, *x.shape)), axis, 0, 0, tiled=True)


def gathered_copies(x, axis, dim):
    return in_order(sent_to_all(x, axis), dim)


def split_up(x, dim, count):
    before, after = (x.shape[:dim], x.shape[dim + 1 :])
    return jnp.moveaxis(x.reshape(*before, count, -1, *after), dim, 0)


def piece_ends(length, count):
    unit = 8 if length >= 8 * count else 1
    return [length // unit * k // count * unit for k in range(1, count)]


def exchange_in_pieces(x, axis, pieces, split_dim, concat_dim):
    parts = split_up(x, split_dim, lax.axis_size(axis))
    split_at = max(range(1, max(2, parts.ndim - 1)), key=lambda d: parts.shape[d])
    outs = []
    for section in jnp.split(parts, piece_ends(parts.shape[split_at], pieces), axis=split_at):
        if section.size:
            outs.append(lax.all_to_all(section, axis, split_axis=0, concat_axis=0, tiled=True))
    return in_order(jnp.concatenate(outs, axis=split_at), concat_dim)


def interpolate_row(source, starts, weight_row, width):
    outputs = []
    for instance in range(source.shape[0]):
        summed = jnp.zeros(source.shape[1:3] + (width,), jnp.float32)
        for member in range(weight_row.shape[0]):
            piece = lax.dynamic_slice_in_dim(source[instance], starts[instance, member], width, 2)
            summed = summed + weight_row[member][None, None, :] * piece
        outputs.append(summed)
    return jnp.stack(outputs)


def on_device(donor_state, time_shift, face_shift, weights, offsets):
    inst_dev = donor_state.shape[1]
    pitch_dev = donor_state.shape[4]
    inst_pad = inst_dev * lax.axis_size("inst")
    period = pitch_dev * lax.axis_size("pitch")
    count = time_shift.shape[1]
    padded = jnp.zeros((2, inst_pad, inst_pad), jnp.float32).at[:, :count, :count].set(time_shift)
    my_first = lax.axis_index("inst") * inst_dev
    swapped = donor_state[::-1]
    local = jnp.einsum(
        "rmk,rkvsp->rmvsp",
        padded,
        lax.all_to_all(swapped, "inst", split_axis=3, concat_axis=1, tiled=True),
        precision=lax.Precision.HIGHEST,
    )
    resampled = lax.all_to_all(local, "inst", split_axis=1, concat_axis=3, tiled=True)
    global_ids = jnp.minimum(my_first + jnp.arange(inst_dev, dtype=jnp.int32), count - 1)
    shifts = face_shift[global_ids]

    def starts_for(row, base, wrap_len):
        values = base + (1 - 2 * row) * shifts[:, None] + offsets[row][None, :]
        values = jnp.mod(values, wrap_len)
        return values

    weight_whole = gathered_copies(weights, "pitch", 2)
    block = lax.all_to_all(resampled, "pitch", split_axis=3, concat_axis=4, tiled=True)
    doubled = jnp.concatenate([block, block], axis=4)
    rows_out = [
        interpolate_row(doubled[row], starts_for(row, 0, period), weight_whole[row], period)
        for row in range(2)
    ]
    received = exchange_in_pieces(jnp.stack(rows_out), "pitch", 2, 4, 3)
    received = jnp.where(
        (my_first + jnp.arange(inst_dev))[None, :, None, None, None] < count, received, 0.0
    )
    return received


def solution(mesh):
    return jax.shard_map(
        on_device,
        mesh=mesh,
        in_specs=(P(None, "inst", None, "span", "pitch"), P(), P(), P(None, None, "pitch"), P()),
        out_specs=P(None, "inst", None, "span", "pitch"),
        check_vma=False,
    )
```

profile of v0, /device:TPU:32, one launch (start us, length us, event | category | flops | bytes accessed | tf_op | source)
XLA Modules:
  0.0 182.2 jit_solution(16522565117469237647)
XLA Ops:
  0.0 2.0 %copy.40 = f32[2,3,5,64,128]{4,0,2,1,3:T(2,128)S(1)} copy(f32[2,3,5,64,128]{4,3,2,1,0:T(8,128)} %param.7) | data formatting | bytes 1966080 | tf_op args[0]
  2.0 5.0 %rev.3 = f32[2,3,5,64,128]{4,0,2,1,3:T(2,128)} reverse(f32[2,3,5,64,128]{4,0,2,1,3:T(2,128)S(1)} %copy.40), dimensions={0} | reverse | bytes 1966080 | tf_op jit(solution)/shard_map/rev | solution.py:61
  7.0 4.5 %all-to-all-start.1 = ((f32[2,3,5,64,128]{4,0,2,1,3:T(2,128)}), f32[2,3,5,64,128]{4,0,2,1,3:T(2,128)S(1)}, u32[]{:S(2)}, u32[]{:S(2)}) async-start(f32[2,3,5,64,128]{4,0,2,1,3:T(2,128)} %rev.3), calls=%async_computation.1 | async-start | bytes 1966080 | tf_op jit(solution)/shard_map/all_to_all | solution.py:65
  11.5 15.2 %all-to-all-done.1 = f32[2,3,5,64,128]{4,0,2,1,3:T(2,128)S(1)} async-done(((f32[2,3,5,64,128]{4,0,2,1,3:T(2,128)}), f32[2,3,5,64,128]{4,0,2,1,3:T(2,128)S(1)}, u32[]{:S(2)}, u32[]{:S(2)}) %all-to-all-start.1) | async-done | bytes 983072 | tf_op jit(solution)/shard_map/all_to_all | solution.py:65
  26.7 0.1 copy.61
  26.9 1.0 fusion
  27.9 0.2 copy.44
  28.1 17.8 %all_to_all.69 = f32[2,24,5,8,128]{4,3,2,0,1:T(8,128)S(1)} all-to-all(f32[2,24,5,8,128]{4,3,2,0,1:T(8,128)S(1)} %copy.44), channel_id=1, replica_groups=mesh['pitch'=16,'inst'=8,'span'=2] {'inst'}, dimensions={1} | all-to-all | bytes 1966080 | tf_op jit(solution)/shard_map/all_to_all | solution.py:68
  45.9 0.6 broadcast_in_dim.11
  46.6 11.0 %all-to-all-start = ((f32[16,2,4,128]{3,2,1,0:T(4,128)}), f32[16,2,4,128]{3,2,1,0:T(4,128)S(1)}, u32[]{:S(2)}, u32[]{:S(2)}) async-start(f32[16,2,4,128]{3,2,1,0:T(4,128)} %broadcast_in_dim.11), calls=%async_computation | async-start | bytes 131072 | tf_op jit(solution)/shard_map/all_to_all | solution.py:15
  57.6 0.1 copy.59
  57.7 1.7 copy.47
  59.4 7.3 %all-to-all-done = f32[16,2,4,128]{3,2,1,0:T(4,128)S(1)} async-done(((f32[16,2,4,128]{3,2,1,0:T(4,128)}), f32[16,2,4,128]{3,2,1,0:T(4,128)S(1)}, u32[]{:S(2)}, u32[]{:S(2)}) %all-to-all-start) | async-done | bytes 65568 | tf_op jit(solution)/shard_map/all_to_all | solution.py:15
  66.7 4.4 %all-to-all-start.3 = ((f32[2,3,5,64,128]{4,0,2,1,3:T(2,128)}), f32[2,3,5,64,128]{4,0,2,1,3:T(2,128)S(1)}, u32[]{:S(2)}, u32[]{:S(2)}) async-start(f32[2,3,5,64,128]{4,0,2,1,3:T(2,128)} %copy.47), calls=%async_computation.3 | async-start | bytes 1966080 | tf_op jit(solution)/shard_map/all_to_all | solution.py:78
  71.2 0.6 gather_fusion
  71.9 0.7 fusion.11
  87.5 0.7 fusion.10
  117.8 0.2 copy.60
  118.0 0.3 all_to_all.60
  118.4 0.1 constant_dynamic-update-slice_fusion
  118.6 0.1 fusion.8
  118.7 0.4 constant_dynamic-slice_fusion.11
  119.2 0.1 dynamic_slice.151
  119.5 0.4 constant_dynamic-slice_fusion.7
  120.3 0.4 constant_dynamic-slice_fusion.3
  121.1 1.1 constant_dynamic-slice_fusion.23
  122.2 1.0 dynamic_slice.127
  123.5 1.2 constant_dynamic-slice_fusion.19
  124.6 1.0 dynamic_slice.135
  125.7 1.0 dynamic_slice.131
  126.7 1.7 dynamic_slice.129
  128.4 1.2 constant_dynamic-slice_fusion.15
  129.6 1.0 dynamic_slice.143
  130.7 1.7 dynamic_slice.141
  132.3 1.7 dynamic_slice.139
  134.0 1.7 dynamic_slice.137
  135.6 0.2 multiply_add_fusion.2
  135.8 0.7 copy-done.2
  136.7 0.2 multiply_add_fusion.5
  137.0 0.9 copy.49
  137.9 9.7 %all-to-all-start.4 = ((f32[16,2,3,2,4,128]{5,4,3,2,1,0:T(4,128)}), f32[16,2,3,2,4,128]{5,4,3,2,1,0:T(4,128)S(1)}, u32[]{:S(2)}, u32[]{:S(2)}) async-start(f32[16,2,3,2,4,128]{5,4,3,2,1,0:T(4,128)} %copy.49), calls=%async_computation.4 | async-start | bytes 786432 | tf_op jit(solution)/shard_map/all_to_all | solution.py:38
  147.7 1.0 copy.50
  148.7 11.1 %all-to-all-done.4 = f32[16,2,3,2,4,128]{5,4,3,2,1,0:T(4,128)S(1)} async-done(((f32[16,2,3,2,4,128]{5,4,3,2,1,0:T(4,128)}), f32[16,2,3,2,4,128]{5,4,3,2,1,0:T(4,128)S(1)}, u32[]{:S(2)}, u32[]{:S(2)}) %all-to-all-start.4) | async-done | bytes 393248 | tf_op jit(solution)/shard_map/all_to_all | solution.py:38
  159.8 4.8 %all-to-all-start.5 = ((f32[16,2,3,3,4,128]{5,4,3,2,1,0:T(4,128)}), f32[16,2,3,3,4,128]{5,4,3,2,1,0:T(4,128)S(1)}, u32[]{:S(2)}, u32[]{:S(2)}) async-start(f32[16,2,3,3,4,128]{5,4,3,2,1,0:T(4,128)} %copy.50), calls=%async_computation.5 | async-start | bytes 1179648 | tf_op jit(solution)/shard_map/all_to_all | solution.py:38
  164.7 15.9 %all-to-all-done.5 = f32[16,2,3,3,4,128]{5,4,3,2,1,0:T(4,128)S(1)} async-done(((f32[16,2,3,3,4,128]{5,4,3,2,1,0:T(4,128)}), f32[16,2,3,3,4,128]{5,4,3,2,1,0:T(4,128)S(1)}, u32[]{:S(2)}, u32[]{:S(2)}) %all-to-all-start.5) | async-done | bytes 589856 | tf_op jit(solution)/shard_map/all_to_all | solution.py:38
  180.6 0.2 maximum_bitcast_fusion.1
  180.8 0.3 copy.51
  181.1 1.1 broadcast_select_fusion
  (44 shorter events, 1.9 us)
Async XLA Ops:
  0.0 71.2 %copy-start = (s32[17]{0:T(128)S(1)}, s32[17]{0:T(128)}, u32[]{:S(2)}) copy-start(s32[17]{0:T(128)} %param.9) | copy-start | bytes 208
  2.0 9.5 %copy-start.5 = (f32[2,17,17]{2,0,1:T(2,128)S(1)}, f32[2,17,17]{2,0,1:T(2,128)}, u32[]{:S(2)}) copy-start(f32[2,17,17]{2,0,1:T(2,128)} %param.8) | copy-start | bytes 6940
  7.0 19.7 %all-to-all-start.1 = ((f32[2,3,5,64,128]{4,0,2,1,3:T(2,128)}), f32[2,3,5,64,128]{4,0,2,1,3:T(2,128)S(1)}, u32[]{:S(2)}, u32[]{:S(2)}) async-start(f32[2,3,5,64,128]{4,0,2,1,3:T(2,128)} %rev.3), calls=%async_computation.1 | async-start | bytes 1966080 | tf_op jit(solution)/shard_map/all_to_all | solution.py:65
  27.9 18.0 %copy-start.6 = (f32[2,4,128]{2,1,0:T(4,128)S(1)}, f32[2,4,128]{2,1,0:T(4,128)}, u32[]{:S(2)}) copy-start(f32[2,4,128]{2,1,0:T(4,128)} %param.10) | copy-start | bytes 12292
  46.6 20.2 %all-to-all-start = ((f32[16,2,4,128]{3,2,1,0:T(4,128)}), f32[16,2,4,128]{3,2,1,0:T(4,128)S(1)}, u32[]{:S(2)}, u32[]{:S(2)}) async-start(f32[16,2,4,128]{3,2,1,0:T(4,128)} %broadcast_in_dim.11), calls=%async_computation | async-start | bytes 131072 | tf_op jit(solution)/shard_map/all_to_all | solution.py:15
  57.7 14.1 %copy-start.7 = (s32[2,4]{1,0:T(2,128)S(1)}, s32[2,4]{1,0:T(2,128)}, u32[]{:S(2)}) copy-start(s32[2,4]{1,0:T(2,128)} %param.11) | copy-start | bytes 100
  66.7 51.1 %all-to-all-start.3 = ((f32[2,3,5,64,128]{4,0,2,1,3:T(2,128)}), f32[2,3,5,64,128]{4,0,2,1,3:T(2,128)S(1)}, u32[]{:S(2)}, u32[]{:S(2)}) async-start(f32[2,3,5,64,128]{4,0,2,1,3:T(2,128)} %copy.47), calls=%async_computation.3 | async-start | bytes 1966080 | tf_op jit(solution)/shard_map/all_to_all | solution.py:78
  129.6 6.2 %copy-start.1 = (f32[1,1,5,4,16,128]{5,4,1,3,2,0:T(8,128)S(1)}, f32[1,1,5,4,16,128]{5,4,1,3,2,0:T(8,128)}, u32[]{:S(2)}) copy-start(f32[1,1,5,4,16,128]{5,4,1,3,2,0:T(8,128)} %dynamic_slice.129) | copy-start | bytes 491524
  135.6 0.9 copy-start.2
  135.6 1.0 copy-start.3
  135.6 1.1 copy-start.4
  137.9 21.9 %all-to-all-start.4 = ((f32[16,2,3,2,4,128]{5,4,3,2,1,0:T(4,128)}), f32[16,2,3,2,4,128]{5,4,3,2,1,0:T(4,128)S(1)}, u32[]{:S(2)}, u32[]{:S(2)}) async-start(f32[16,2,3,2,4,128]{5,4,3,2,1,0:T(4,128)} %copy.49), calls=%async_computation.4 | async-start | bytes 786432 | tf_op jit(solution)/shard_map/all_to_all | solution.py:38
  159.8 20.7 %all-to-all-start.5 = ((f32[16,2,3,3,4,128]{5,4,3,2,1,0:T(4,128)}), f32[16,2,3,3,4,128]{5,4,3,2,1,0:T(4,128)S(1)}, u32[]{:S(2)}, u32[]{:S(2)}) async-start(f32[16,2,3,3,4,128]{5,4,3,2,1,0:T(4,128)} %copy.50), calls=%async_computation.5 | async-start | bytes 1179648 | tf_op jit(solution)/shard_map/all_to_all | solution.py:38
where the time goes:
time: 184 us; the launch traced here: 182 us
  waiting for transfers between devices  49.5 us (27%)
  between operations  44.8 us (24%)
  starting transfers between devices  34.5 us (19%)
  local copies, waits for them, and re-layouts  32.7 us (18%)
  blocking collectives  17.8 us (10%)
  other arithmetic  1.88 us (1%)
    all_to_all x2, waiting for transfers between devices, exchange_in_pieces(): lax.all_to_all(section, axis, split_axis=0, concat_axis=0, tiled=True)  27 us
    all_to_all x1, blocking collectives, on_device(): lax.all_to_all(local, 'inst', split_axis=1, concat_axis=3, tiled=True)  17.8 us
    dynamic_slice x30, local copies, waits for them, and re-layouts, interpolate_row(): lax.dynamic_slice_in_dim(source[instance], starts[instance, member], widt...  16.8 us
    all_to_all x1, waiting for transfers between devices, on_device(): lax.all_to_all(swapped, 'inst', split_axis=3, concat_axis=1, tiled=True)  15.2 us
    all_to_all x2, starting transfers between devices, exchange_in_pieces(): lax.all_to_all(section, axis, split_axis=0, concat_axis=0, tiled=True)  14.5 us
    all_to_all x1, starting transfers between devices, sent_to_all(): lax.all_to_all(jnp.broadcast_to(x[None], (count, *x.shape)), axis, 0, 0,...  11 us
    all_to_all x1, waiting for transfers between devices, sent_to_all(): lax.all_to_all(jnp.broadcast_to(x[None], (count, *x.shape)), axis, 0, 0,...  7.28 us
    rev x1, local copies, waits for them, and re-layouts, on_device(): swapped = donor_state[::-1]  5 us
  transfers between devices with their start and end apart: 5, of which 4 were waited for; matrix products, arithmetic and copies ran while one was open for 3% of the time, Pallas kernels for 0%

commit v1 on v0

v1 whole, which is shorter than its diff:
```python
import functools

import jax
import jax.numpy as jnp
from jax import lax
from jax.experimental import pallas as pl
from jax.experimental.pallas import tpu as pltpu
from jax.sharding import PartitionSpec as P

VARS = 5
ROWS = 16
VMEM = pl.BlockSpec(memory_space=pltpu.VMEM)
SMEM = pl.BlockSpec(memory_space=pltpu.SMEM)


def pack_kernel(donor_ref, weights_ref, sent_ref):
    inst_dev, span = donor_ref.shape[1], donor_ref.shape[3]
    members = weights_ref.shape[1]
    member = lax.rem(lax.axis_index("inst"), members)
    for r in range(2):
        first = r * span * ROWS
        for k in range(inst_dev):
            for v in range(VARS):
                sent_ref[pl.ds(first + k * VARS + v, span, stride=ROWS), :] = donor_ref[1 - r, k, v]
        row = weights_ref[r, pl.ds(member, 1), :]
        sent_ref[pl.ds(first + ROWS - 1, span, stride=ROWS), :] = jnp.broadcast_to(row, (span, row.shape[1]))


def mixing_matrix(matrix, inst_dev, rows, cols):
    count = matrix.shape[0]
    high = lax.Precision.HIGHEST
    row_id = lax.broadcasted_iota(jnp.int32, (rows, count), 0)
    pick_row = (row_id // 8 == lax.broadcasted_iota(jnp.int32, (rows, count), 1)).astype(jnp.float32)
    col_id = lax.broadcasted_iota(jnp.int32, (count, cols), 1)
    source = (col_id // ROWS) * inst_dev + lax.rem(col_id, ROWS) // VARS
    pick_col = (source == lax.broadcasted_iota(jnp.int32, (count, cols), 0)).astype(jnp.float32)
    spread = jnp.dot(
        pick_row,
        jnp.dot(matrix, pick_col, precision=high, preferred_element_type=jnp.float32),
        precision=high,
        preferred_element_type=jnp.float32,
    )
    row_id = lax.broadcasted_iota(jnp.int32, (rows, cols), 0)
    col_id = lax.rem(lax.broadcasted_iota(jnp.int32, (rows, cols), 1), ROWS)
    row_var = lax.rem(lax.rem(row_id, 8) + 8 * VARS - VARS * lax.rem(row_id // 8, inst_dev), 8)
    keep = (row_var == lax.rem(col_id, VARS)) & (col_id < inst_dev * VARS)
    return jnp.where(keep, spread, 0.0)


def transfer_kernel(
    inst_dev, blocks, got_ref, time_shift_ref, face_shift_ref, offsets_ref, sent_ref, mixed_ref, weight_ref
):
    members = offsets_ref.shape[1]
    count = time_shift_ref.shape[1]
    lanes = got_ref.shape[1]
    depth = got_ref.shape[0] // blocks
    owners = depth // ROWS
    position = lax.axis_index("pitch") * owners + lax.axis_index("inst")
    row = position // (blocks * owners // 2)
    sign = 1 - 2 * row
    mix = mixing_matrix(time_shift_ref[row], inst_dev, count * 8, depth)
    for block in range(blocks):
        part = jnp.dot(
            mix,
            got_ref[block * depth : (block + 1) * depth, :],
            precision=lax.Precision.HIGHEST,
            preferred_element_type=jnp.float32,
        )
        mixed_ref[block] = part
        mixed_ref[block + blocks] = part
        for member in range(members):
            at = block * depth + member * ROWS + ROWS - 1
            weight_ref[member, block] = jnp.broadcast_to(got_ref[at : at + 1, :], (8, lanes))
    lane = lax.broadcasted_iota(jnp.int32, (1, 1, lanes), 2)
    sub = lax.broadcasted_iota(jnp.int32, (1, 8, 1), 1)

    def interpolated(m):
        total = jnp.zeros((blocks, 8, lanes), jnp.float32)
        for member in range(members):
            start = sign * face_shift_ref[m] + offsets_ref[row, member] + blocks * lanes
            start = lax.rem(start, blocks * lanes)
            skip, turn = start // lanes, lax.rem(start, lanes)
            window = mixed_ref[pl.ds(skip, blocks + 1), m * 8 : (m + 1) * 8, :]
            turned = pltpu.roll(window.reshape((blocks + 1) * 8, lanes), lax.rem(lanes - turn, lanes), 1)
            turned = turned.reshape(blocks + 1, 8, lanes)
            moved = jnp.where(lane < lanes - turn, turned[:blocks], turned[1:])
            total = total + weight_ref[member] * moved
        return total

    zero = jnp.zeros((blocks, 8, lanes), jnp.float32)
    for owner in range(owners):
        parts = [interpolated(m) if m < count else zero for m in range(owner * inst_dev, (owner + 1) * inst_dev)]
        low = jnp.where(sub < VARS, parts[0], parts[1])
        high = jnp.where(sub < 2 * VARS - 8, parts[1], parts[2])
        sent_ref[:, owner * ROWS : owner * ROWS + 8, :] = low
        sent_ref[:, owner * ROWS + 8 : (owner + 1) * ROWS, :] = high


def unpack_kernel(got_ref, received_ref):
    inst_dev, span = received_ref.shape[1], received_ref.shape[3]
    for r in range(2):
        for k in range(inst_dev):
            for v in range(VARS):
                at = r * span * ROWS + k * VARS + v
                received_ref[r, k, v] = got_ref[pl.ds(at, span, stride=ROWS), :]


def on_device(donor_state, time_shift, face_shift, weights, offsets):
    inst_dev, lanes = donor_state.shape[1], donor_state.shape[4]
    blocks, owners = lax.axis_size("pitch"), lax.axis_size("inst")
    peers = blocks * owners
    members = weights.shape[1]
    flat = jax.ShapeDtypeStruct((peers * ROWS, lanes), jnp.float32)

    def exchanged(x):
        whole = x.reshape(peers, ROWS, lanes)
        return lax.all_to_all(whole, ("pitch", "inst"), 0, 0, tiled=True).reshape(flat.shape)

    packed = pl.pallas_call(pack_kernel, out_shape=flat, in_specs=[VMEM, VMEM], out_specs=VMEM)(donor_state, weights)
    got = exchanged(packed)
    sent = pl.pallas_call(
        functools.partial(transfer_kernel, inst_dev, blocks),
        out_shape=jax.ShapeDtypeStruct((blocks, owners * ROWS, lanes), jnp.float32),
        in_specs=[VMEM, VMEM, SMEM, SMEM],
        out_specs=VMEM,
        scratch_shapes=[
            pltpu.VMEM((2 * blocks, time_shift.shape[1] * 8, lanes), jnp.float32),
            pltpu.VMEM((members, blocks, 8, lanes), jnp.float32),
        ],
        compiler_params=pltpu.CompilerParams(vmem_limit_bytes=24 * 2**20),
    )(got, time_shift, face_shift, offsets)
    back = exchanged(sent)
    return pl.pallas_call(
        unpack_kernel,
        out_shape=jax.ShapeDtypeStruct(donor_state.shape, jnp.float32),
        in_specs=[VMEM],
        out_specs=VMEM,
    )(back)


def solution(mesh):
    return jax.shard_map(
        on_device,
        mesh=mesh,
        in_specs=(P(None, "inst", None, "span", "pitch"), P(), P(), P(None, None, "pitch"), P()),
        out_specs=P(None, "inst", None, "span", "pitch"),
        check_vma=False,
    )
```

time: 184 us -> 97.2 us (0.53)
  the two profiles are of different devices: /device:TPU:32 before, /device:TPU:1 now
where the time goes in v1:
time: 97.2 us; the launch traced here: 96.9 us
  blocking collectives  37.9 us (39%)
  waiting for transfers between devices  33.1 us (34%)
  starting transfers between devices  16.5 us (17%)
  Pallas kernels  9.37 us (10%)
    all_to_all x1, blocking collectives, exchanged(): lax.all_to_all(whole, ('pitch', 'inst'), 0, 0, tiled=True)  37.9 us
    all_to_all x1, waiting for transfers between devices, exchanged(): lax.all_to_all(whole, ('pitch', 'inst'), 0, 0, tiled=True)  33.1 us
    all_to_all x1, starting transfers between devices, exchanged(): lax.all_to_all(whole, ('pitch', 'inst'), 0, 0, tiled=True)  16.5 us
    pallas_call x1, Pallas kernels, on_device(): pl.pallas_call(functools.partial(transfer_kernel, inst_dev, blocks), out_...  4.23 us
    pallas_call x1, Pallas kernels, on_device(): pl.pallas_call(pack_kernel, out_shape=flat, in_specs=[VMEM, VMEM], out_sp...  2.68 us
    pallas_call x1, Pallas kernels, on_device(): pl.pallas_call(unpack_kernel, out_shape=jax.ShapeDtypeStruct(donor_state....  2.47 us
  transfers between devices with their start and end apart: 1, of which 1 were waited for; matrix products, arithmetic and copies ran while one was open for 0% of the time, Pallas kernels for 0%

profile of v1, /device:TPU:1, one launch (start us, length us, event | category | flops | bytes accessed | tf_op | source)
XLA Modules:
  0.0 96.9 jit_solution(14096699470350224940)
XLA Ops:
  0.0 2.7 %shard_map.55 = f32[2048,128]{1,0:T(8,128)} custom-call(f32[2,3,5,64,128]{4,3,2,1,0:T(8,128)} %donor_ref.1, f32[2,4,128]{2,1,0:T(4,128)} %weights_ref.1), custom_call_target="tpu_custom_call" | custom-call | tf_op jit(solution)/shard_map/pallas_call | solution.py:119
  2.7 0.0 copy-start.2
  2.7 16.5 %all-to-all-start = ((f32[128,16,128]{2,1,0:T(8,128)}), f32[128,16,128]{2,1,0:T(8,128)S(1)}, u32[]{:S(2)}, u32[]{:S(2)}) async-start(f32[128,16,128]{2,1,0:T(8,128)} %bitcast.6), calls=%async_computation | async-start | bytes 2097152 | tf_op jit(solution)/shard_map/all_to_all | solution.py:117
  19.2 0.0 copy-done.2
  19.2 0.0 copy-start
  19.3 0.0 copy-start.1
  19.3 33.1 %all-to-all-done = f32[128,16,128]{2,1,0:T(8,128)S(1)} async-done(((f32[128,16,128]{2,1,0:T(8,128)}), f32[128,16,128]{2,1,0:T(8,128)S(1)}, u32[]{:S(2)}, u32[]{:S(2)}) %all-to-all-start) | async-done | bytes 1048608 | tf_op jit(solution)/shard_map/all_to_all | solution.py:117
  52.4 0.0 copy-done
  52.4 0.0 copy-done.1
  52.4 4.2 %shard_map.56 = f32[16,128,128]{2,1,0:T(8,128)S(1)} custom-call(f32[2048,128]{1,0:T(8,128)S(1)} %bitcast.4, f32[2,17,17]{2,1,0:T(8,128)S(1)} %copy.6.time_shift_ref, s32[17]{0:T(128)S(1)} %copy-done.1, s32[2,4]{1,0:T(2,128)S(1)} %copy-done), custom_call_target="tpu_custom_call" | custom-call | tf_op jit(solution)/shard_map/pallas_call | solution.py:121
  56.6 37.9 %all_to_all.10 = f32[128,16,128]{2,1,0:T(8,128)} all-to-all(f32[128,16,128]{2,1,0:T(8,128)S(1)} %bitcast.5), channel_id=1, replica_groups=mesh['pitch'=16,'inst'=8,'span'=2] {'pitch','inst'}, dimensions={0} | all-to-all | bytes 2097152 | tf_op jit(solution)/shard_map/all_to_all | solution.py:117
  94.5 2.5 %shard_map.57 = f32[2,3,5,64,128]{4,3,2,1,0:T(8,128)} custom-call(f32[2048,128]{1,0:T(8,128)} %bitcast.7), custom_call_target="tpu_custom_call" | custom-call | tf_op jit(solution)/shard_map/pallas_call | solution.py:133
  (1 shorter events, 0.0 us)
Async XLA Ops:
  2.7 16.5 %copy-start.2 = (f32[2,17,17]{2,0,1:T(2,128)S(1)}, f32[2,17,17]{2,0,1:T(2,128)}, u32[]{:S(2)}) copy-start(f32[2,17,17]{2,0,1:T(2,128)} %param.6) | copy-start | bytes 6940
  2.7 49.7 %all-to-all-start = ((f32[128,16,128]{2,1,0:T(8,128)}), f32[128,16,128]{2,1,0:T(8,128)S(1)}, u32[]{:S(2)}, u32[]{:S(2)}) async-start(f32[128,16,128]{2,1,0:T(8,128)} %bitcast.6), calls=%async_computation | async-start | bytes 2097152 | tf_op jit(solution)/shard_map/all_to_all | solution.py:117
  19.2 33.1 %copy-start = (s32[2,4]{1,0:T(2,128)S(1)}, s32[2,4]{1,0:T(2,128)}, u32[]{:S(2)}) copy-start(s32[2,4]{1,0:T(2,128)} %offsets_ref.1) | copy-start | bytes 100
  19.3 33.1 %copy-start.1 = (s32[17]{0:T(128)S(1)}, s32[17]{0:T(128)}, u32[]{:S(2)}) copy-start(s32[17]{0:T(128)} %face_shift_ref.1) | copy-start | bytes 208

commit v2 on v1

v2 whole, which is shorter than its diff:
```python
import functools

import jax
import jax.numpy as jnp
from jax import lax
from jax.experimental import pallas as pl
from jax.experimental.pallas import tpu as pltpu
from jax.sharding import PartitionSpec as P

VARS = 5
SUB = 8
VMEM = pl.BlockSpec(memory_space=pltpu.VMEM)
SMEM = pl.BlockSpec(memory_space=pltpu.SMEM)


def params(mib):
    return pltpu.CompilerParams(vmem_limit_bytes=mib * 2**20)


def ceil_to(value, unit):
    return -(-value // unit) * unit


def mixing_matrix(matrix, inst_dev, rows, cols):
    count = matrix.shape[0]
    high = lax.Precision.HIGHEST
    row_id = lax.broadcasted_iota(jnp.int32, (rows, count), 0)
    pick_row = (row_id // SUB == lax.broadcasted_iota(jnp.int32, (rows, count), 1)).astype(jnp.float32)
    col_id = lax.broadcasted_iota(jnp.int32, (count, cols), 1)
    pick_col = (col_id // VARS == lax.broadcasted_iota(jnp.int32, (count, cols), 0)).astype(jnp.float32)
    spread = jnp.dot(
        pick_row,
        jnp.dot(matrix, pick_col, precision=high, preferred_element_type=jnp.float32),
        precision=high,
        preferred_element_type=jnp.float32,
    )
    row_id = lax.broadcasted_iota(jnp.int32, (rows, cols), 0)
    col_var = lax.rem(lax.broadcasted_iota(jnp.int32, (rows, cols), 1), VARS)
    row_var = lax.rem(lax.rem(row_id, SUB) + VARS * SUB * count - VARS * (row_id // SUB), SUB)
    return jnp.where(row_var == col_var, spread, 0.0)


def pack_kernel(half, donor_ref, weights_ref, time_shift_ref, sent_ref, mix_ref):
    inst_dev, span = donor_ref.shape[1], donor_ref.shape[3]
    count = time_shift_ref.shape[1]
    depth = inst_dev * VARS
    row = pl.program_id(0)
    for k in range(inst_dev):
        for v in range(VARS):
            sent_ref[pl.ds(k * VARS + v, span, stride=depth), :] = donor_ref[0, k, v]
    spare = -(-count // inst_dev)

    @pl.when(lax.axis_index("inst") == spare)
    def _():
        for member in range(weights_ref.shape[1]):
            one = weights_ref[row, member : member + 1, :]
            sent_ref[pl.ds(member, span, stride=depth), :] = jnp.broadcast_to(one, (span, one.shape[1]))

    @pl.when(row == 0)
    def _():
        mix_ref[...] = mixing_matrix(time_shift_ref[half()], inst_dev, *mix_ref.shape)


def split(x):
    high = x.astype(jnp.bfloat16)
    return high, (x - high.astype(jnp.float32)).astype(jnp.bfloat16)


def transfer_kernel(half, inst_dev, blocks, got_ref, mix_ref, face_shift_ref, offsets_ref, sent_ref, mixed_ref, weight_ref):
    members = offsets_ref.shape[1]
    count = face_shift_ref.shape[0]
    lanes = got_ref.shape[1]
    depth = got_ref.shape[0] // blocks
    period = blocks * lanes
    spare = -(-count // inst_dev) * inst_dev * VARS
    row = half()
    sign = 1 - 2 * row
    used = mix_ref.shape[1]
    mix_high, mix_low = split(mix_ref[...])
    mix = jnp.concatenate([mix_high, mix_high, mix_low], axis=1)
    for block in range(blocks):
        high, low = split(got_ref[block * depth : block * depth + used, :])
        part = jnp.dot(mix, jnp.concatenate([high, low, high], axis=0), preferred_element_type=jnp.float32)
        mixed_ref[block] = part
        mixed_ref[block + blocks] = part
        for member in range(members):
            at = block * depth + spare + member
            weight_ref[member, block] = jnp.broadcast_to(got_ref[at : at + 1, :], (SUB, lanes))
    lane = lax.broadcasted_iota(jnp.int32, (1, 1, lanes), 2)
    sub = lax.broadcasted_iota(jnp.int32, (1, SUB, 1), 1)

    def interpolated(m):
        total = None
        for member in range(members):
            start = lax.rem(sign * face_shift_ref[m] + offsets_ref[row, member] + period, period)
            skip, turn = start // lanes, lax.rem(start, lanes)
            window = mixed_ref[pl.ds(skip, blocks + 1), m * SUB : (m + 1) * SUB, :]
            turned = pltpu.roll(window.reshape((blocks + 1) * SUB, lanes), lax.rem(lanes - turn, lanes), 1)
            turned = turned.reshape(blocks + 1, SUB, lanes)
            term = weight_ref[member] * jnp.where(lane < lanes - turn, turned[:blocks], turned[1:])
            total = term if total is None else total + term
        return total

    parts = {}
    for tile in range(depth // SUB):
        first, last = tile * SUB // VARS, (tile * SUB + SUB - 1) // VARS
        joined = None
        for m in range(first, last + 1):
            if m >= count:
                part = jnp.zeros((blocks, SUB, lanes), jnp.float32)
            else:
                if m not in parts:
                    parts = {m - 1: parts[m - 1], m: interpolated(m)} if m - 1 in parts else {m: interpolated(m)}
                part = parts[m]
            joined = part if joined is None else jnp.where(sub >= m * VARS - tile * SUB, part, joined)
        sent_ref[:, tile * SUB : (tile + 1) * SUB, :] = joined


def unpack_kernel(got_ref, received_ref):
    inst_dev, span = received_ref.shape[1], received_ref.shape[3]
    depth = inst_dev * VARS
    first = pl.program_id(0) * span * depth
    for k in range(inst_dev):
        for v in range(VARS):
            received_ref[0, k, v] = got_ref[pl.ds(first + k * VARS + v, span, stride=depth), :]


def my_row(peers, owners):
    return (lax.axis_index("pitch") * owners + lax.axis_index("inst")) // (peers // 2)


def on_device(donor_state, time_shift, face_shift, weights, offsets, blocks=None, owners=None, exchange=None):
    _, inst_dev, _, span, lanes = donor_state.shape
    blocks, owners = blocks or lax.axis_size("pitch"), owners or lax.axis_size("inst")
    peers = blocks * owners
    members, count = weights.shape[1], time_shift.shape[1]
    depth = inst_dev * VARS
    used = ceil_to(count * VARS, SUB)
    half = functools.partial(my_row, peers, owners)

    def exchanged(x):
        whole = x.reshape(peers, depth, 1, lanes)
        return lax.all_to_all(whole, ("pitch", "inst"), 0, 0, tiled=True).reshape(peers * depth, lanes)

    exchanged = exchange or exchanged

    packed, mix = pl.pallas_call(
        functools.partial(pack_kernel, half),
        grid=(2,),
        out_shape=(
            jax.ShapeDtypeStruct((peers * depth, lanes), jnp.float32),
            jax.ShapeDtypeStruct((count * SUB, used), jnp.float32),
        ),
        in_specs=[
            pl.BlockSpec((1, inst_dev, VARS, span, lanes), lambda r: (1 - r, 0, 0, 0, 0)),
            VMEM,
            VMEM,
        ],
        out_specs=(pl.BlockSpec((span * depth, lanes), lambda r: (r, 0)), VMEM),
        compiler_params=params(8),
    )(donor_state, weights, time_shift)
    got = exchanged(packed)
    sent = pl.pallas_call(
        functools.partial(transfer_kernel, half, inst_dev, blocks),
        out_shape=jax.ShapeDtypeStruct((blocks, owners * depth, lanes), jnp.float32),
        in_specs=[VMEM, VMEM, SMEM, SMEM],
        out_specs=VMEM,
        scratch_shapes=[
            pltpu.VMEM((2 * blocks, count * SUB, lanes), jnp.float32),
            pltpu.VMEM((members, blocks, SUB, lanes), jnp.float32),
        ],
        compiler_params=params(24),
    )(got, mix, face_shift, offsets)
    back = exchanged(sent)
    return pl.pallas_call(
        unpack_kernel,
        grid=(2,),
        out_shape=jax.ShapeDtypeStruct(donor_state.shape, jnp.float32),
        in_specs=[VMEM],
        out_specs=pl.BlockSpec((1, inst_dev, VARS, span, lanes), lambda r: (r, 0, 0, 0, 0)),
        compiler_params=params(8),
    )(back)


def solution(mesh):
    return jax.shard_map(
        on_device,
        mesh=mesh,
        in_specs=(P(None, "inst", None, "span", "pitch"), P(), P(), P(None, None, "pitch"), P()),
        out_specs=P(None, "inst", None, "span", "pitch"),
        check_vma=False,
    )
```

time: 97.2 us -> 91.4 us (0.940)
  blocking collectives: 37.9 us -> 84.2 us
  waiting for transfers between devices: 33.1 us -> 0 us
  starting transfers between devices: 16.5 us -> 0 us
  Pallas kernels: 9.37 us -> 4.3 us
  local copies, waits for them, and re-layouts: 0.02 us -> 2.62 us
    all_to_all x1 -> x2, blocking collectives: 37.9 us -> 84.2 us  [exchanged(): lax.all_to_all(whole, ('pitch', 'inst'), 0, 0, tiled=True)]
    all_to_all x1 -> x0, waiting for transfers between devices: 33.1 us -> none  [exchanged(): lax.all_to_all(whole, ('pitch', 'inst'), 0, 0, tiled=True)]
    all_to_all x1 -> x0, starting transfers between devices: 16.5 us -> none  [exchanged(): lax.all_to_all(whole, ('pitch', 'inst'), 0, 0, tiled=True)]
    pallas_call x3, Pallas kernels: 9.37 us -> 4.3 us  [the longest x1 2.78 us: on_device(): pl.pallas_call(functools.partial(transfer_kernel, half, inst_dev, blocks)...]
    unnamed x7 -> x9, local copies, waits for them, and re-layouts: 0.02 us -> 2.62 us
  transfers between devices with their start and end apart: 1 -> 0, of which waited for: 1 -> 0; matrix products, arithmetic and copies ran while one was open for 0% -> 0% of each run, Pallas kernels for 0% -> 0%
where the time goes in v2:
time: 91.4 us; the launch traced here: 91.2 us
  blocking collectives  84.2 us (92%)
  Pallas kernels  4.3 us (5%)
  local copies, waits for them, and re-layouts  2.62 us (3%)
    all_to_all x2, blocking collectives, exchanged(): lax.all_to_all(whole, ('pitch', 'inst'), 0, 0, tiled=True)  84.2 us
    pallas_call x1, Pallas kernels, on_device(): pl.pallas_call(functools.partial(transfer_kernel, half, inst_dev, blocks)...  2.78 us
    unnamed x9, local copies, waits for them, and re-layouts  2.62 us

profile of v2, /device:TPU:1, one launch (start us, length us, event | category | flops | bytes accessed | tf_op | source)
XLA Modules:
  0.0 91.2 jit_solution(10439600191205593195)
XLA Ops:
  0.0 0.0 copy-start.1
  0.0 0.7 copy.8.time_shift_ref
  0.7 0.0 copy-done.1
  0.7 0.0 copy-start
  0.7 1.2 %copy-done = f32[2,3,5,64,128]{4,3,2,1,0:T(8,128)S(1)} copy-done((f32[2,3,5,64,128]{4,3,2,1,0:T(8,128)S(1)}, f32[2,3,5,64,128]{4,3,2,1,0:T(8,128)}, u32[]{:S(2)}) %copy-start) | copy-done | bytes 983064
  1.9 0.5 shard_map.55
  2.5 47.9 %all_to_all.10 = f32[128,15,1,128]{3,2,1,0:T(1,128)S(1)} all-to-all(f32[128,15,1,128]{3,2,1,0:T(1,128)S(1)} %bitcast.7), channel_id=1, replica_groups=mesh['pitch'=16,'inst'=8,'span'=2] {'pitch','inst'}, dimensions={0} | all-to-all | bytes 1966080 | tf_op jit(solution)/shard_map/all_to_all | solution.py:143
  50.4 0.0 copy-start.2
  50.4 0.0 copy-start.3
  50.4 0.7 copy-done.2
  51.1 0.0 copy-done.3
  51.1 2.8 %shard_map.56 = f32[16,120,128]{2,1,0:T(8,128)S(1)} custom-call(f32[1920,128]{1,0:T(8,128)S(1)} %bitcast.4, f32[136,88]{1,0:T(8,128)S(1)} %get-tuple-element.8.mix_ref, s32[17]{0:T(128)S(1)} %copy-done.3, s32[2,4]{1,0:T(2,128)S(1)} %copy-done.2), custom_call_target="tpu_custom_call" | custom-call | tf_op jit(solution)/shard_map/pallas_call | solution.py:163
  53.9 36.3 %all_to_all.11 = f32[128,15,1,128]{3,2,1,0:T(1,128)S(1)} all-to-all(f32[128,15,1,128]{3,2,1,0:T(1,128)S(1)} %bitcast.5), channel_id=1, replica_groups=mesh['pitch'=16,'inst'=8,'span'=2] {'pitch','inst'}, dimensions={0} | all-to-all | bytes 1966080 | tf_op jit(solution)/shard_map/all_to_all | solution.py:143
  90.2 1.0 %shard_map.57 = f32[2,3,5,64,128]{4,3,2,1,0:T(8,128)} custom-call(f32[1920,128]{1,0:T(8,128)S(1)} %bitcast.6), custom_call_target="tpu_custom_call" | custom-call | tf_op jit(solution)/shard_map/pallas_call | solution.py:175
Async XLA Ops:
  0.0 0.7 copy-start.1
  0.7 1.2 %copy-start = (f32[2,3,5,64,128]{4,3,2,1,0:T(8,128)S(1)}, f32[2,3,5,64,128]{4,3,2,1,0:T(8,128)}, u32[]{:S(2)}) copy-start(f32[2,3,5,64,128]{4,3,2,1,0:T(8,128)} %donor_ref.1) | copy-start | bytes 2949124
  50.4 0.7 copy-start.2
  50.4 0.7 copy-start.3

commit v3 on v2

--- a/solution.py
+++ b/solution.py
@@ -8,6 +8,7 @@
 from jax.sharding import PartitionSpec as P
 
 VARS = 5
+CUTS = 2
 SUB = 8
 VMEM = pl.BlockSpec(memory_space=pltpu.VMEM)
 SMEM = pl.BlockSpec(memory_space=pltpu.SMEM)
@@ -40,25 +41,50 @@
     return jnp.where(row_var == col_var, spread, 0.0)
 
 
-def pack_kernel(half, donor_ref, weights_ref, time_shift_ref, sent_ref, mix_ref):
+def pack_kernel(count, donor_ref, weights_ref, sent_ref, held, weights, packed, weights_sem, in_sems, out_sems):
     inst_dev, span = donor_ref.shape[1], donor_ref.shape[3]
-    count = time_shift_ref.shape[1]
     depth = inst_dev * VARS
-    row = pl.program_id(0)
-    for k in range(inst_dev):
-        for v in range(VARS):
-            sent_ref[pl.ds(k * VARS + v, span, stride=depth), :] = donor_ref[0, k, v]
-    spare = -(-count // inst_dev)
-
-    @pl.when(lax.axis_index("inst") == spare)
-    def _():
-        for member in range(weights_ref.shape[1]):
-            one = weights_ref[row, member : member + 1, :]
-            sent_ref[pl.ds(member, span, stride=depth), :] = jnp.broadcast_to(one, (span, one.shape[1]))
-
-    @pl.when(row == 0)
-    def _():
-        mix_ref[...] = mixing_matrix(time_shift_ref[half()], inst_dev, *mix_ref.shape)
+    step = span // CUTS
+    fetched = pltpu.make_async_copy(weights_ref, weights, weights_sem)
+    pieces = [(r, c) for r in range(2) for c in range(CUTS)]
+
+    def arrival(r, c):
+        part = pl.ds(c * step, step)
+        return pltpu.make_async_copy(donor_ref.at[1 - r, :, :, part], held.at[r, :, :, part], in_sems.at[r, c])
+
+    def departure(r, c):
+        part = pl.ds((r * span + c * step) * depth, step * depth)
+        return pltpu.make_async_copy(packed.at[part], sent_ref.at[part], out_sems.at[r, c])
+
+    for r, c in pieces:
+        arrival(r, c).start()
+    fetched.start()
+    fetched.wait()
+    spare = lax.axis_index("inst") == -(-count // inst_dev)
+    for r, c in pieces:
+        arrival(r, c).wait()
+        first = (r * span + c * step) * depth
+        for k in range(inst_dev):
+            for v in range(VARS):
+                faces = held[r, k, v, c * step : (c + 1) * step]
+                member = k * VARS + v
+                if member < weights.shape[1]:
+                    faces = jnp.where(spare, weights[r, member : member + 1, :], faces)
+                packed[pl.ds(first + member, step, stride=depth), :] = faces
+        departure(r, c).start()
+    for r, c in pieces:
+        departure(r, c).wait()
+
+
+def prepare_kernel(half, inst_dev, period, time_shift_ref, face_shift_ref, offsets_ref, mix_ref, starts_ref):
+    row = half()
+    sign = 1 - 2 * row
+    count, members = face_shift_ref.shape[0], offsets_ref.shape[1]
+    for m in range(count):
+        for member in range(members):
+            start = sign * face_shift_ref[m] + offsets_ref[row, member]
+            starts_ref[m * members + member] = jnp.where(start < 0, start + period, start)
+    mix_ref[...] = mixing_matrix(time_shift_ref[row], inst_dev, *mix_ref.shape)
 
 
 def split(x):
@@ -66,23 +92,23 @@
     return high, (x - high.astype(jnp.float32)).astype(jnp.bfloat16)
 
 
-def transfer_kernel(half, inst_dev, blocks, got_ref, mix_ref, face_shift_ref, offsets_ref, sent_ref, mixed_ref, weight_ref):
-    members = offsets_ref.shape[1]
-    count = face_shift_ref.shape[0]
+def transfer_kernel(inst_dev, blocks, members, got_ref, mix_ref, starts_ref, sent_ref, mixed_ref, weight_ref):
+    count = starts_ref.shape[0] // members
     lanes = got_ref.shape[1]
     depth = got_ref.shape[0] // blocks
-    period = blocks * lanes
     spare = -(-count // inst_dev) * inst_dev * VARS
-    row = half()
-    sign = 1 - 2 * row
     used = mix_ref.shape[1]
     mix_high, mix_low = split(mix_ref[...])
-    mix = jnp.concatenate([mix_high, mix_high, mix_low], axis=1)
+    mix = jnp.concatenate([mix_high, mix_high], axis=1)
     for block in range(blocks):
-        high, low = split(got_ref[block * depth : block * depth + used, :])
-        part = jnp.dot(mix, jnp.concatenate([high, low, high], axis=0), preferred_element_type=jnp.float32)
-        mixed_ref[block] = part
-        mixed_ref[block + blocks] = part
+        if block % 2 == 0:
+            two = [got_ref[b * depth : b * depth + used, :] for b in (block, block + 1)]
+            high, low = split(jnp.concatenate(two, axis=1))
+            part = jnp.dot(mix, jnp.concatenate([high, low], axis=0), preferred_element_type=jnp.float32) + jnp.dot(mix_low, high, preferred_element_type=jnp.float32)
+            for b in range(2):
+                one = part[:, b * lanes : (b + 1) * lanes]
+                mixed_ref[block + b] = one
+                mixed_ref[block + b + blocks] = one
         for member in range(members):
             at = block * depth + spare + member
             weight_ref[member, block] = jnp.broadcast_to(got_ref[at : at + 1, :], (SUB, lanes))
@@ -92,7 +118,7 @@
     def interpolated(m):
         total = None
         for member in range(members):
-            start = lax.rem(sign * face_shift_ref[m] + offsets_ref[row, member] + period, period)
+            start = starts_ref[m * members + member]
             skip, turn = start // lanes, lax.rem(start, lanes)
             window = mixed_ref[pl.ds(skip, blocks + 1), m * SUB : (m + 1) * SUB, :]
             turned = pltpu.roll(window.reshape((blocks + 1) * SUB, lanes), lax.rem(lanes - turn, lanes), 1)
@@ -144,33 +170,44 @@
 
     exchanged = exchange or exchanged
 
-    packed, mix = pl.pallas_call(
-        functools.partial(pack_kernel, half),
-        grid=(2,),
+    hbm = pl.BlockSpec(memory_space=pltpu.HBM)
+    packed = pl.pallas_call(
+        functools.partial(pack_kernel, count),
+        out_shape=jax.ShapeDtypeStruct((peers * depth, lanes), jnp.float32),
+        in_specs=[hbm] * 2,
+        out_specs=hbm,
+        scratch_shapes=[
+            pltpu.VMEM(donor_state.shape, jnp.float32),
+            pltpu.VMEM(weights.shape, jnp.float32),
+            pltpu.VMEM((peers * depth, lanes), jnp.float32),
+            pltpu.SemaphoreType.DMA(()),
+            pltpu.SemaphoreType.DMA((2, CUTS)),
+            pltpu.SemaphoreType.DMA((2, CUTS)),
+        ],
+        compiler_params=params(56),
+    )(donor_state, weights)
+    mix, starts = pl.pallas_call(
+        functools.partial(prepare_kernel, half, inst_dev, blocks * lanes),
         out_shape=(
-            jax.ShapeDtypeStruct((peers * depth, lanes), jnp.float32),
             jax.ShapeDtypeStruct((count * SUB, used), jnp.float32),
+            jax.ShapeDtypeStruct((count * members,), jnp.int32),
         ),
-        in_specs=[
-            pl.BlockSpec((1, inst_dev, VARS, span, lanes), lambda r: (1 - r, 0, 0, 0, 0)),
-            VMEM,
-            VMEM,
-        ],
-        out_specs=(pl.BlockSpec((span * depth, lanes), lambda r: (r, 0)), VMEM),
+        in_specs=[VMEM, SMEM, SMEM],
+        out_specs=(VMEM, SMEM),
         compiler_params=params(8),
-    )(donor_state, weights, time_shift)
+    )(time_shift, face_shift, offsets)
     got = exchanged(packed)
     sent = pl.pallas_call(
-        functools.partial(transfer_kernel, half, inst_dev, blocks),
+        functools.partial(transfer_kernel, inst_dev, blocks, members),
         out_shape=jax.ShapeDtypeStruct((blocks, owners * depth, lanes), jnp.float32),
-        in_specs=[VMEM, VMEM, SMEM, SMEM],
+        in_specs=[VMEM, VMEM, SMEM],
         out_specs=VMEM,
         scratch_shapes=[
             pltpu.VMEM((2 * blocks, count * SUB, lanes), jnp.float32),
             pltpu.VMEM((members, blocks, SUB, lanes), jnp.float32),
         ],
         compiler_params=params(24),
-    )(got, mix, face_shift, offsets)
+    )(got, mix, starts)
     back = exchanged(sent)
     return pl.pallas_call(
         unpack_kernel,

time: 91.4 us -> 90.3 us (0.988)
  blocking collectives: 84.2 us -> 36.3 us
  waiting for transfers between devices: 0 us -> 29.8 us
  starting transfers between devices: 0 us -> 16.4 us
  Pallas kernels: 4.3 us -> 6.78 us
  local copies, waits for them, and re-layouts: 2.62 us -> 0.67 us
    all_to_all x2 -> x1, blocking collectives: 84.2 us -> 36.3 us  [exchanged(): lax.all_to_all(whole, ('pitch', 'inst'), 0, 0, tiled=True)]
    all_to_all x0 -> x1, waiting for transfers between devices: none -> 29.8 us  [exchanged(): lax.all_to_all(whole, ('pitch', 'inst'), 0, 0, tiled=True)]
    all_to_all x0 -> x1, starting transfers between devices: none -> 16.4 us  [exchanged(): lax.all_to_all(whole, ('pitch', 'inst'), 0, 0, tiled=True)]
    pallas_call x2 -> x3, Pallas kernels: 3.33 us -> 5.81 us  [the longest x1 2.38 us: on_device(): pl.pallas_call(functools.partial(transfer_kernel, inst_dev, blocks, membe...]
    unnamed x9 -> x7, local copies, waits for them, and re-layouts: 2.62 us -> 0.67 us
  transfers between devices with their start and end apart: 0 -> 1, of which waited for: 0 -> 1; matrix products, arithmetic and copies ran while one was open for 0% -> 0% of each run, Pallas kernels for 0% -> 1%
where the time goes in v3:
time: 90.3 us; the launch traced here: 90 us
  blocking collectives  36.3 us (40%)
  waiting for transfers between devices  29.8 us (33%)
  starting transfers between devices  16.4 us (18%)
  Pallas kernels  6.78 us (8%)
    all_to_all x1, blocking collectives, exchanged(): lax.all_to_all(whole, ('pitch', 'inst'), 0, 0, tiled=True)  36.3 us
    all_to_all x1, waiting for transfers between devices, exchanged(): lax.all_to_all(whole, ('pitch', 'inst'), 0, 0, tiled=True)  29.8 us
    all_to_all x1, starting transfers between devices, exchanged(): lax.all_to_all(whole, ('pitch', 'inst'), 0, 0, tiled=True)  16.4 us
    pallas_call x1, Pallas kernels, on_device(): pl.pallas_call(functools.partial(transfer_kernel, inst_dev, blocks, membe...  2.38 us
    pallas_call x1, Pallas kernels, on_device(): pl.pallas_call(functools.partial(pack_kernel, count), out_shape=jax.Shape...  2.14 us
  transfers between devices with their start and end apart: 1, of which 1 were waited for; matrix products, arithmetic and copies ran while one was open for 0% of the time, Pallas kernels for 1%

profile of v3, /device:TPU:1, one launch (start us, length us, event | category | flops | bytes accessed | tf_op | source)
XLA Modules:
  0.0 90.0 jit_solution(5832941896897652904)
XLA Ops:
  0.0 2.1 %shard_map.55 = f32[1920,128]{1,0:T(8,128)} custom-call(f32[2,3,5,64,128]{4,3,2,1,0:T(8,128)} %donor_ref.1, f32[2,4,128]{2,1,0:T(4,128)} %weights_ref.1), custom_call_target="tpu_custom_call" | custom-call | tf_op jit(solution)/shard_map/pallas_call | solution.py:174
  2.2 0.0 copy-start.2
  2.2 16.4 %all-to-all-start = ((f32[128,15,1,128]{3,2,1,0:T(1,128)}), f32[128,15,1,128]{3,2,1,0:T(1,128)S(1)}, u32[]{:S(2)}, u32[]{:S(2)}) async-start(f32[128,15,1,128]{3,2,1,0:T(1,128)} %bitcast.7), calls=%async_computation | async-start | bytes 1966080 | tf_op jit(solution)/shard_map/all_to_all | solution.py:169
  18.6 0.0 copy-done.2
  18.6 0.0 copy-start
  18.6 0.0 copy-start.1
  18.6 0.6 copy-done
  19.3 0.0 copy-done.1
  19.3 1.3 %shard_map.56 = (f32[136,88]{1,0:T(8,128)S(1)}, s32[68]{0:T(128)S(1)}) custom-call(f32[2,17,17]{2,1,0:T(8,128)S(1)} %copy.9.time_shift_ref, s32[17]{0:T(128)S(1)} %copy-done.1, s32[2,4]{1,0:T(2,128)S(1)} %copy-done), custom_call_target="tpu_custom_call" | custom-call | tf_op jit(solution)/shard_map/pallas_call | solution.py:189
  20.6 29.8 %all-to-all-done = f32[128,15,1,128]{3,2,1,0:T(1,128)S(1)} async-done(((f32[128,15,1,128]{3,2,1,0:T(1,128)}), f32[128,15,1,128]{3,2,1,0:T(1,128)S(1)}, u32[]{:S(2)}, u32[]{:S(2)}) %all-to-all-start) | async-done | bytes 983072 | tf_op jit(solution)/shard_map/all_to_all | solution.py:169
  50.3 2.4 %shard_map.57 = f32[16,120,128]{2,1,0:T(8,128)S(1)} custom-call(f32[1920,128]{1,0:T(8,128)S(1)} %bitcast.4, f32[136,88]{1,0:T(8,128)S(1)} %get-tuple-element.7.mix_ref, s32[68]{0:T(128)S(1)} %get-tuple-element.8.starts_ref), custom_call_target="tpu_custom_call" | custom-call | tf_op jit(solution)/shard_map/pallas_call | solution.py:200
  52.7 36.3 %all_to_all.10 = f32[128,15,1,128]{3,2,1,0:T(1,128)S(1)} all-to-all(f32[128,15,1,128]{3,2,1,0:T(1,128)S(1)} %bitcast.5), channel_id=1, replica_groups=mesh['pitch'=16,'inst'=8,'span'=2] {'pitch','inst'}, dimensions={0} | all-to-all | bytes 1966080 | tf_op jit(solution)/shard_map/all_to_all | solution.py:169
  89.0 1.0 %shard_map.58 = f32[2,3,5,64,128]{4,3,2,1,0:T(8,128)} custom-call(f32[1920,128]{1,0:T(8,128)S(1)} %bitcast.6), custom_call_target="tpu_custom_call" | custom-call | tf_op jit(solution)/shard_map/pallas_call | solution.py:212
  (1 shorter events, 0.0 us)
Async XLA Ops:
  2.2 16.4 %copy-start.2 = (f32[2,17,17]{2,0,1:T(2,128)S(1)}, f32[2,17,17]{2,0,1:T(2,128)}, u32[]{:S(2)}) copy-start(f32[2,17,17]{2,0,1:T(2,128)} %param.6) | copy-start | bytes 6940
  2.2 48.2 %all-to-all-start = ((f32[128,15,1,128]{3,2,1,0:T(1,128)}), f32[128,15,1,128]{3,2,1,0:T(1,128)S(1)}, u32[]{:S(2)}, u32[]{:S(2)}) async-start(f32[128,15,1,128]{3,2,1,0:T(1,128)} %bitcast.7), calls=%async_computation | async-start | bytes 1966080 | tf_op jit(solution)/shard_map/all_to_all | solution.py:169
  18.6 0.7 copy-start
  18.6 0.7 copy-start.1

commit v4 on v3

--- a/solution.py
+++ b/solution.py
@@ -22,22 +22,21 @@
     return -(-value // unit) * unit
 
 
-def mixing_matrix(matrix, inst_dev, rows, cols):
+def mixing_matrix(matrix, size):
     count = matrix.shape[0]
     high = lax.Precision.HIGHEST
-    row_id = lax.broadcasted_iota(jnp.int32, (rows, count), 0)
-    pick_row = (row_id // SUB == lax.broadcasted_iota(jnp.int32, (rows, count), 1)).astype(jnp.float32)
-    col_id = lax.broadcasted_iota(jnp.int32, (count, cols), 1)
-    pick_col = (col_id // VARS == lax.broadcasted_iota(jnp.int32, (count, cols), 0)).astype(jnp.float32)
+
+    def picks(shape, dim):
+        own = lax.broadcasted_iota(jnp.int32, shape, dim) // VARS
+        return (own == lax.broadcasted_iota(jnp.int32, shape, 1 - dim)).astype(jnp.float32)
+
     spread = jnp.dot(
-        pick_row,
-        jnp.dot(matrix, pick_col, precision=high, preferred_element_type=jnp.float32),
+        picks((size, count), 0),
+        jnp.dot(matrix, picks((count, size), 1), precision=high, preferred_element_type=jnp.float32),
         precision=high,
         preferred_element_type=jnp.float32,
     )
-    row_id = lax.broadcasted_iota(jnp.int32, (rows, cols), 0)
-    col_var = lax.rem(lax.broadcasted_iota(jnp.int32, (rows, cols), 1), VARS)
-    row_var = lax.rem(lax.rem(row_id, SUB) + VARS * SUB * count - VARS * (row_id // SUB), SUB)
+    row_var, col_var = (lax.rem(lax.broadcasted_iota(jnp.int32, (size, size), d), VARS) for d in range(2))
     return jnp.where(row_var == col_var, spread, 0.0)
 
 
@@ -76,15 +75,17 @@
         departure(r, c).wait()
 
 
-def prepare_kernel(half, inst_dev, period, time_shift_ref, face_shift_ref, offsets_ref, mix_ref, starts_ref):
+def prepare_kernel(half, lanes, period, time_shift_ref, face_shift_ref, offsets_ref, mix_ref, starts_ref):
     row = half()
     sign = 1 - 2 * row
     count, members = face_shift_ref.shape[0], offsets_ref.shape[1]
     for m in range(count):
         for member in range(members):
             start = sign * face_shift_ref[m] + offsets_ref[row, member]
-            starts_ref[m * members + member] = jnp.where(start < 0, start + period, start)
-    mix_ref[...] = mixing_matrix(time_shift_ref[row], inst_dev, *mix_ref.shape)
+            start = jnp.where(start < 0, start + period, start)
+            starts_ref[m * members + member] = lax.div(start, lanes)
+            starts_ref[(count + m) * members + member] = lax.rem(start, lanes)
+    mix_ref[...] = mixing_matrix(time_shift_ref[row], mix_ref.shape[0])
 
 
 def split(x):
@@ -92,54 +93,44 @@
     return high, (x - high.astype(jnp.float32)).astype(jnp.bfloat16)
 
 
-def transfer_kernel(inst_dev, blocks, members, got_ref, mix_ref, starts_ref, sent_ref, mixed_ref, weight_ref):
-    count = starts_ref.shape[0] // members
+def transfer_kernel(inst_dev, blocks, members, got_ref, mix_ref, table_ref, sent_ref, mixed_ref, starts_ref, sem):
+    table = pltpu.make_async_copy(table_ref, starts_ref, sem)
+    table.start()
+    count = starts_ref.shape[0] // (2 * members)
     lanes = got_ref.shape[1]
     depth = got_ref.shape[0] // blocks
-    spare = -(-count // inst_dev) * inst_dev * VARS
-    used = mix_ref.shape[1]
+    twice = 2 * blocks + 1
+    used = mix_ref.shape[0]
     mix_high, mix_low = split(mix_ref[...])
     mix = jnp.concatenate([mix_high, mix_high], axis=1)
+    for block in range(0, blocks, 2):
+        high, low = split(jnp.concatenate([got_ref[b * depth : b * depth + used, :] for b in (block, block + 1)], axis=1))
+        part = jnp.dot(mix, jnp.concatenate([high, low], axis=0), preferred_element_type=jnp.float32)
+        part = part + jnp.dot(mix_low, high, preferred_element_type=jnp.float32)
+        for b in range(2):
+            one = part[:, b * lanes : (b + 1) * lanes]
+            for copy in range(2):
+                mixed_ref[pl.ds(block + b + copy * blocks, used, stride=twice), :] = one
+    table.wait()
+    first_spare = -(-count // inst_dev) * inst_dev * VARS
+    weights = [got_ref[pl.ds(first_spare + member, blocks, stride=depth), :] for member in range(members)]
+    lane = lax.broadcasted_iota(jnp.int32, (blocks, lanes), 1)
+    for m in range(count):
+        totals = [None] * VARS
+        for member in range(members):
+            skip, turn = starts_ref[m * members + member], starts_ref[(count + m) * members + member]
+            back = jnp.where(turn == 0, 0, lanes - turn)
+            here = lane >= turn
+            for v in range(VARS):
+                at = (m * VARS + v) * twice + skip
+                faces = jnp.where(here, mixed_ref[pl.ds(at, blocks), :], mixed_ref[pl.ds(at + 1, blocks), :])
+                term = weights[member] * pltpu.roll(faces, back, 1)
+                totals[v] = term if member == 0 else totals[v] + term
+        for v in range(VARS):
+            sent_ref[pl.ds(m * VARS + v, blocks, stride=depth), :] = totals[v]
+    none = jnp.zeros((depth - count * VARS, lanes), jnp.float32)
     for block in range(blocks):
-        if block % 2 == 0:
-            two = [got_ref[b * depth : b * depth + used, :] for b in (block, block + 1)]
-            high, low = split(jnp.concatenate(two, axis=1))
-            part = jnp.dot(mix, jnp.concatenate([high, low], axis=0), preferred_element_type=jnp.float32) + jnp.dot(mix_low, high, preferred_element_type=jnp.float32)
-            for b in range(2):
-                one = part[:, b * lanes : (b + 1) * lanes]
-                mixed_ref[block + b] = one
-                mixed_ref[block + b + blocks] = one
-        for member in range(members):
-            at = block * depth + spare + member
-            weight_ref[member, block] = jnp.broadcast_to(got_ref[at : at + 1, :], (SUB, lanes))
-    lane = lax.broadcasted_iota(jnp.int32, (1, 1, lanes), 2)
-    sub = lax.broadcasted_iota(jnp.int32, (1, SUB, 1), 1)
-
-    def interpolated(m):
-        total = None
-        for member in range(members):
-            start = starts_ref[m * members + member]
-            skip, turn = start // lanes, lax.rem(start, lanes)
-            window = mixed_ref[pl.ds(skip, blocks + 1), m * SUB : (m + 1) * SUB, :]
-            turned = pltpu.roll(window.reshape((blocks + 1) * SUB, lanes), lax.rem(lanes - turn, lanes), 1)
-            turned = turned.reshape(blocks + 1, SUB, lanes)
-            term = weight_ref[member] * jnp.where(lane < lanes - turn, turned[:blocks], turned[1:])
-            total = term if total is None else total + term
-        return total
-
-    parts = {}
-    for tile in range(depth // SUB):
-        first, last = tile * SUB // VARS, (tile * SUB + SUB - 1) // VARS
-        joined = None
-        for m in range(first, last + 1):
-            if m >= count:
-                part = jnp.zeros((blocks, SUB, lanes), jnp.float32)
-            else:
-                if m not in parts:
-                    parts = {m - 1: parts[m - 1], m: interpolated(m)} if m - 1 in parts else {m: interpolated(m)}
-                part = parts[m]
-            joined = part if joined is None else jnp.where(sub >= m * VARS - tile * SUB, part, joined)
-        sent_ref[:, tile * SUB : (tile + 1) * SUB, :] = joined
+        sent_ref[block * depth + count * VARS : (block + 1) * depth, :] = none
 
 
 def unpack_kernel(got_ref, received_ref):
@@ -187,10 +178,10 @@
         compiler_params=params(56),
     )(donor_state, weights)
     mix, starts = pl.pallas_call(
-        functools.partial(prepare_kernel, half, inst_dev, blocks * lanes),
+        functools.partial(prepare_kernel, half, lanes, blocks * lanes),
         out_shape=(
-            jax.ShapeDtypeStruct((count * SUB, used), jnp.float32),
-            jax.ShapeDtypeStruct((count * members,), jnp.int32),
+            jax.ShapeDtypeStruct((used, used), jnp.float32),
+            jax.ShapeDtypeStruct((2 * count * members,), jnp.int32),
         ),
         in_specs=[VMEM, SMEM, SMEM],
         out_specs=(VMEM, SMEM),
@@ -199,12 +190,13 @@
     got = exchanged(packed)
     sent = pl.pallas_call(
         functools.partial(transfer_kernel, inst_dev, blocks, members),
-        out_shape=jax.ShapeDtypeStruct((blocks, owners * depth, lanes), jnp.float32),
-        in_specs=[VMEM, VMEM, SMEM],
+        out_shape=jax.ShapeDtypeStruct((peers * depth, lanes), jnp.float32),
+        in_specs=[VMEM, VMEM, VMEM],
         out_specs=VMEM,
         scratch_shapes=[
-            pltpu.VMEM((2 * blocks, count * SUB, lanes), jnp.float32),
-            pltpu.VMEM((members, blocks, SUB, lanes), jnp.float32),
+            pltpu.VMEM((used * (2 * blocks + 1), lanes), jnp.float32),
+            pltpu.SMEM((2 * count * members,), jnp.int32),
+            pltpu.SemaphoreType.DMA(()),
         ],
         compiler_params=params(24),
     )(got, mix, starts)

time: 90.3 us -> 89.2 us (0.988)
    pallas_call x1, Pallas kernels: 2.38 us -> 1.35 us  [on_device(): pl.pallas_call(functools.partial(transfer_kernel, inst_dev, blocks, membe...]
  transfers between devices with their start and end apart: 1 -> 1, of which waited for: 1 -> 1; matrix products, arithmetic and copies ran while one was open for 0% -> 0% of each run, Pallas kernels for 1% -> 2%
where the time goes in v4:
time: 89.2 us; the launch traced here: 88.9 us
  blocking collectives  36.3 us (41%)
  waiting for transfers between devices  29.6 us (33%)
  starting transfers between devices  16.4 us (18%)
  Pallas kernels  5.94 us (7%)
    all_to_all x1, blocking collectives, exchanged(): lax.all_to_all(whole, ('pitch', 'inst'), 0, 0, tiled=True)  36.3 us
    all_to_all x1, waiting for transfers between devices, exchanged(): lax.all_to_all(whole, ('pitch', 'inst'), 0, 0, tiled=True)  29.6 us
    all_to_all x1, starting transfers between devices, exchanged(): lax.all_to_all(whole, ('pitch', 'inst'), 0, 0, tiled=True)  16.4 us
    pallas_call x1, Pallas kernels, on_device(): pl.pallas_call(functools.partial(pack_kernel, count), out_shape=jax.Shape...  2.14 us
  transfers between devices with their start and end apart: 1, of which 1 were waited for; matrix products, arithmetic and copies ran while one was open for 0% of the time, Pallas kernels for 2%

profile of v4, /device:TPU:1, one launch (start us, length us, event | category | flops | bytes accessed | tf_op | source)
XLA Modules:
  0.0 88.9 jit_solution(10176076699297371086)
XLA Ops:
  0.0 2.1 %shard_map.55 = f32[1920,128]{1,0:T(8,128)} custom-call(f32[2,3,5,64,128]{4,3,2,1,0:T(8,128)} %donor_ref.1, f32[2,4,128]{2,1,0:T(4,128)} %weights_ref.1), custom_call_target="tpu_custom_call" | custom-call | tf_op jit(solution)/shard_map/pallas_call | solution.py:165
  2.2 0.0 copy-start.2
  2.2 16.4 %all-to-all-start = ((f32[128,15,1,128]{3,2,1,0:T(1,128)}), f32[128,15,1,128]{3,2,1,0:T(1,128)S(1)}, u32[]{:S(2)}, u32[]{:S(2)}) async-start(f32[128,15,1,128]{3,2,1,0:T(1,128)} %bitcast.7), calls=%async_computation | async-start | bytes 1966080 | tf_op jit(solution)/shard_map/all_to_all | solution.py:160
  18.6 0.0 copy-done.2
  18.6 0.0 copy-start
  18.6 0.0 copy-start.1
  18.6 0.6 copy-done
  19.3 0.0 copy-done.1
  19.3 1.5 %shard_map.56 = (f32[88,88]{1,0:T(8,128)S(1)}, s32[136]{0:T(256)S(1)}) custom-call(f32[2,17,17]{2,1,0:T(8,128)S(1)} %copy.9.time_shift_ref, s32[17]{0:T(128)S(1)} %copy-done.1, s32[2,4]{1,0:T(2,128)S(1)} %copy-done), custom_call_target="tpu_custom_call" | custom-call | tf_op jit(solution)/shard_map/pallas_call | solution.py:180
  20.8 29.6 %all-to-all-done = f32[128,15,1,128]{3,2,1,0:T(1,128)S(1)} async-done(((f32[128,15,1,128]{3,2,1,0:T(1,128)}), f32[128,15,1,128]{3,2,1,0:T(1,128)S(1)}, u32[]{:S(2)}, u32[]{:S(2)}) %all-to-all-start) | async-done | bytes 983072 | tf_op jit(solution)/shard_map/all_to_all | solution.py:160
  50.3 1.3 %shard_map.57 = f32[1920,128]{1,0:T(8,128)S(1)} custom-call(f32[1920,128]{1,0:T(8,128)S(1)} %bitcast.4, f32[88,88]{1,0:T(8,128)S(1)} %get-tuple-element.7.mix_ref, s32[136]{0:T(256)S(1)} %get-tuple-element.8.table_ref), custom_call_target="tpu_custom_call" | custom-call | tf_op jit(solution)/shard_map/pallas_call | solution.py:191
  51.7 36.3 %all_to_all.10 = f32[128,15,1,128]{3,2,1,0:T(1,128)S(1)} all-to-all(f32[128,15,1,128]{3,2,1,0:T(1,128)S(1)} %bitcast.5), channel_id=1, replica_groups=mesh['pitch'=16,'inst'=8,'span'=2] {'pitch','inst'}, dimensions={0} | all-to-all | bytes 1966080 | tf_op jit(solution)/shard_map/all_to_all | solution.py:160
  88.0 1.0 %shard_map.58 = f32[2,3,5,64,128]{4,3,2,1,0:T(8,128)} custom-call(f32[1920,128]{1,0:T(8,128)S(1)} %bitcast.6), custom_call_target="tpu_custom_call" | custom-call | tf_op jit(solution)/shard_map/pallas_call | solution.py:204
  (1 shorter events, 0.0 us)
Async XLA Ops:
  2.2 16.4 %copy-start.2 = (f32[2,17,17]{2,0,1:T(2,128)S(1)}, f32[2,17,17]{2,0,1:T(2,128)}, u32[]{:S(2)}) copy-start(f32[2,17,17]{2,0,1:T(2,128)} %param.6) | copy-start | bytes 6940
  2.2 48.2 %all-to-all-start = ((f32[128,15,1,128]{3,2,1,0:T(1,128)}), f32[128,15,1,128]{3,2,1,0:T(1,128)S(1)}, u32[]{:S(2)}, u32[]{:S(2)}) async-start(f32[128,15,1,128]{3,2,1,0:T(1,128)} %bitcast.7), calls=%async_computation | async-start | bytes 1966080 | tf_op jit(solution)/shard_map/all_to_all | solution.py:160
  18.6 0.7 copy-start
  18.6 0.7 copy-start.1

commit v5 on v4

--- a/solution.py
+++ b/solution.py
@@ -8,8 +8,8 @@
 from jax.sharding import PartitionSpec as P
 
 VARS = 5
-CUTS = 2
-SUB = 8
+CUTS = 1
+TILE = 16
 VMEM = pl.BlockSpec(memory_space=pltpu.VMEM)
 SMEM = pl.BlockSpec(memory_space=pltpu.SMEM)
 
@@ -102,10 +102,10 @@
     twice = 2 * blocks + 1
     used = mix_ref.shape[0]
     mix_high, mix_low = split(mix_ref[...])
-    mix = jnp.concatenate([mix_high, mix_high], axis=1)
     for block in range(0, blocks, 2):
         high, low = split(jnp.concatenate([got_ref[b * depth : b * depth + used, :] for b in (block, block + 1)], axis=1))
-        part = jnp.dot(mix, jnp.concatenate([high, low], axis=0), preferred_element_type=jnp.float32)
+        part = jnp.dot(mix_high, high, preferred_element_type=jnp.float32)
+        part = part + jnp.dot(mix_high, low, preferred_element_type=jnp.float32)
         part = part + jnp.dot(mix_low, high, preferred_element_type=jnp.float32)
         for b in range(2):
             one = part[:, b * lanes : (b + 1) * lanes]
@@ -152,7 +152,7 @@
     peers = blocks * owners
     members, count = weights.shape[1], time_shift.shape[1]
     depth = inst_dev * VARS
-    used = ceil_to(count * VARS, SUB)
+    used = ceil_to(count * VARS, TILE)
     half = functools.partial(my_row, peers, owners)
 
     def exchanged(x):

time: 89.2 us -> 89.1 us (level)
  no operation moved by 1% of the time
where the time goes in v5:
time: 89.1 us; the launch traced here: 88.8 us
  blocking collectives  36.3 us (41%)
  waiting for transfers between devices  29.6 us (33%)
  starting transfers between devices  16.4 us (18%)
  Pallas kernels  5.84 us (7%)
    all_to_all x1, blocking collectives, exchanged(): lax.all_to_all(whole, ('pitch', 'inst'), 0, 0, tiled=True)  36.3 us
    all_to_all x1, waiting for transfers between devices, exchanged(): lax.all_to_all(whole, ('pitch', 'inst'), 0, 0, tiled=True)  29.6 us
    all_to_all x1, starting transfers between devices, exchanged(): lax.all_to_all(whole, ('pitch', 'inst'), 0, 0, tiled=True)  16.4 us
    pallas_call x1, Pallas kernels, on_device(): pl.pallas_call(functools.partial(pack_kernel, count), out_shape=jax.Shape...  2.04 us
  transfers between devices with their start and end apart: 1, of which 1 were waited for; matrix products, arithmetic and copies ran while one was open for 0% of the time, Pallas kernels for 2%

profile of v5, /device:TPU:1, one launch (start us, length us, event | category | flops | bytes accessed | tf_op | source)
XLA Modules:
  0.0 88.8 jit_solution(5845529855195703497)
XLA Ops:
  0.0 2.0 %shard_map.55 = f32[1920,128]{1,0:T(8,128)} custom-call(f32[2,3,5,64,128]{4,3,2,1,0:T(8,128)} %donor_ref.1, f32[2,4,128]{2,1,0:T(4,128)} %weights_ref.1), custom_call_target="tpu_custom_call" | custom-call | tf_op jit(solution)/shard_map/pallas_call | solution.py:165
  2.1 0.0 copy-start.2
  2.1 16.4 %all-to-all-start = ((f32[128,15,1,128]{3,2,1,0:T(1,128)}), f32[128,15,1,128]{3,2,1,0:T(1,128)S(1)}, u32[]{:S(2)}, u32[]{:S(2)}) async-start(f32[128,15,1,128]{3,2,1,0:T(1,128)} %bitcast.7), calls=%async_computation | async-start | bytes 1966080 | tf_op jit(solution)/shard_map/all_to_all | solution.py:160
  18.5 0.0 copy-done.2
  18.5 0.0 copy-start
  18.5 0.0 copy-start.1
  18.5 0.6 copy-done
  19.2 0.0 copy-done.1
  19.2 1.5 %shard_map.56 = (f32[96,96]{1,0:T(8,128)S(1)}, s32[136]{0:T(256)S(1)}) custom-call(f32[2,17,17]{2,1,0:T(8,128)S(1)} %copy.9.time_shift_ref, s32[17]{0:T(128)S(1)} %copy-done.1, s32[2,4]{1,0:T(2,128)S(1)} %copy-done), custom_call_target="tpu_custom_call" | custom-call | tf_op jit(solution)/shard_map/pallas_call | solution.py:180
  20.7 29.6 %all-to-all-done = f32[128,15,1,128]{3,2,1,0:T(1,128)S(1)} async-done(((f32[128,15,1,128]{3,2,1,0:T(1,128)}), f32[128,15,1,128]{3,2,1,0:T(1,128)S(1)}, u32[]{:S(2)}, u32[]{:S(2)}) %all-to-all-start) | async-done | bytes 983072 | tf_op jit(solution)/shard_map/all_to_all | solution.py:160
  50.2 1.4 %shard_map.57 = f32[1920,128]{1,0:T(8,128)S(1)} custom-call(f32[1920,128]{1,0:T(8,128)S(1)} %bitcast.4, f32[96,96]{1,0:T(8,128)S(1)} %get-tuple-element.7.mix_ref, s32[136]{0:T(256)S(1)} %get-tuple-element.8.table_ref), custom_call_target="tpu_custom_call" | custom-call | tf_op jit(solution)/shard_map/pallas_call | solution.py:191
  51.6 36.3 %all_to_all.10 = f32[128,15,1,128]{3,2,1,0:T(1,128)S(1)} all-to-all(f32[128,15,1,128]{3,2,1,0:T(1,128)S(1)} %bitcast.5), channel_id=1, replica_groups=mesh['pitch'=16,'inst'=8,'span'=2] {'pitch','inst'}, dimensions={0} | all-to-all | bytes 1966080 | tf_op jit(solution)/shard_map/all_to_all | solution.py:160
  87.9 1.0 %shard_map.58 = f32[2,3,5,64,128]{4,3,2,1,0:T(8,128)} custom-call(f32[1920,128]{1,0:T(8,128)S(1)} %bitcast.6), custom_call_target="tpu_custom_call" | custom-call | tf_op jit(solution)/shard_map/pallas_call | solution.py:204
  (1 shorter events, 0.0 us)
Async XLA Ops:
  2.1 16.4 %copy-start.2 = (f32[2,17,17]{2,0,1:T(2,128)S(1)}, f32[2,17,17]{2,0,1:T(2,128)}, u32[]{:S(2)}) copy-start(f32[2,17,17]{2,0,1:T(2,128)} %param.6) | copy-start | bytes 6940
  2.1 48.2 %all-to-all-start = ((f32[128,15,1,128]{3,2,1,0:T(1,128)}), f32[128,15,1,128]{3,2,1,0:T(1,128)S(1)}, u32[]{:S(2)}, u32[]{:S(2)}) async-start(f32[128,15,1,128]{3,2,1,0:T(1,128)} %bitcast.7), calls=%async_computation | async-start | bytes 1966080 | tf_op jit(solution)/shard_map/all_to_all | solution.py:160
  18.5 0.7 copy-start
  18.5 0.7 copy-start.1

commit v6 on v5

--- a/solution.py
+++ b/solution.py
@@ -115,6 +115,11 @@
     first_spare = -(-count // inst_dev) * inst_dev * VARS
     weights = [got_ref[pl.ds(first_spare + member, blocks, stride=depth), :] for member in range(members)]
     lane = lax.broadcasted_iota(jnp.int32, (blocks, lanes), 1)
+
+    def place(m, v):
+        owner, own = divmod(m * VARS + v, inst_dev * VARS)
+        return pl.ds(owner * blocks * inst_dev * VARS + own, blocks, stride=inst_dev * VARS)
+
     for m in range(count):
         totals = [None] * VARS
         for member in range(members):
@@ -127,19 +132,22 @@
                 term = weights[member] * pltpu.roll(faces, back, 1)
                 totals[v] = term if member == 0 else totals[v] + term
         for v in range(VARS):
-            sent_ref[pl.ds(m * VARS + v, blocks, stride=depth), :] = totals[v]
-    none = jnp.zeros((depth - count * VARS, lanes), jnp.float32)
-    for block in range(blocks):
-        sent_ref[block * depth + count * VARS : (block + 1) * depth, :] = none
-
-
-def unpack_kernel(got_ref, received_ref):
+            sent_ref[place(m, v), :] = totals[v]
+    none = jnp.zeros((blocks, lanes), jnp.float32)
+    for m in range(count, depth // VARS):
+        for v in range(VARS):
+            sent_ref[place(m, v), :] = none
+
+
+def unpack_kernel(blocks, owners, got_ref, received_ref):
     inst_dev, span = received_ref.shape[1], received_ref.shape[3]
     depth = inst_dev * VARS
-    first = pl.program_id(0) * span * depth
-    for k in range(inst_dev):
-        for v in range(VARS):
-            received_ref[0, k, v] = got_ref[pl.ds(first + k * VARS + v, span, stride=depth), :]
+    first = pl.program_id(0) * (span // owners)
+    for c in range(span // owners):
+        for k in range(inst_dev):
+            for v in range(VARS):
+                rows = pl.ds((first + c) * depth + k * VARS + v, owners, stride=blocks * depth)
+                received_ref[0, k, v, c * owners : (c + 1) * owners] = got_ref[rows, :]
 
 
 def my_row(peers, owners):
@@ -155,9 +163,9 @@
     used = ceil_to(count * VARS, TILE)
     half = functools.partial(my_row, peers, owners)
 
-    def exchanged(x):
+    def exchanged(x, axes):
         whole = x.reshape(peers, depth, 1, lanes)
-        return lax.all_to_all(whole, ("pitch", "inst"), 0, 0, tiled=True).reshape(peers * depth, lanes)
+        return lax.all_to_all(whole, axes, 0, 0, tiled=True).reshape(peers * depth, lanes)
 
     exchanged = exchange or exchanged
 
@@ -187,7 +195,7 @@
         out_specs=(VMEM, SMEM),
         compiler_params=params(8),
     )(time_shift, face_shift, offsets)
-    got = exchanged(packed)
+    got = exchanged(packed, ("pitch", "inst"))
     sent = pl.pallas_call(
         functools.partial(transfer_kernel, inst_dev, blocks, members),
         out_shape=jax.ShapeDtypeStruct((peers * depth, lanes), jnp.float32),
@@ -200,9 +208,9 @@
         ],
         compiler_params=params(24),
     )(got, mix, starts)
-    back = exchanged(sent)
+    back = exchanged(sent, ("inst", "pitch"))
     return pl.pallas_call(
-        unpack_kernel,
+        functools.partial(unpack_kernel, blocks, owners),
         grid=(2,),
         out_shape=jax.ShapeDtypeStruct(donor_state.shape, jnp.float32),
         in_specs=[VMEM],

time: 89.1 us -> 86.9 us (0.975)
  blocking collectives: 36.3 us -> 33.6 us
    all_to_all x1, blocking collectives: 36.3 us -> 33.6 us  [exchanged(): lax.all_to_all(whole, axes, 0, 0, tiled=True).reshape(peers * depth, lanes)]
where the time goes in v6:
time: 86.9 us; the launch traced here: 86.3 us
  blocking collectives  33.6 us (39%)
  waiting for transfers between devices  29.6 us (34%)
  starting transfers between devices  16.4 us (19%)
  Pallas kernels  5.96 us (7%)
    all_to_all x1, blocking collectives, exchanged(): lax.all_to_all(whole, axes, 0, 0, tiled=True).reshape(peers * depth, lanes)  33.6 us
    all_to_all x1, waiting for transfers between devices, exchanged(): lax.all_to_all(whole, axes, 0, 0, tiled=True).reshape(peers * depth, lanes)  29.6 us
    all_to_all x1, starting transfers between devices, exchanged(): lax.all_to_all(whole, axes, 0, 0, tiled=True).reshape(peers * depth, lanes)  16.4 us
    pallas_call x1, Pallas kernels, on_device(): pl.pallas_call(functools.partial(pack_kernel, count), out_shape=jax.Shape...  2.04 us
  transfers between devices with their start and end apart: 1, of which 1 were waited for; matrix products, arithmetic and copies ran while one was open for 0% of the time, Pallas kernels for 2%

profile of v6, /device:TPU:1, one launch (start us, length us, event | category | flops | bytes accessed | tf_op | source)
XLA Modules:
  0.0 86.3 jit_solution(17614725746089578418)
XLA Ops:
  0.0 2.0 %shard_map.55 = f32[1920,128]{1,0:T(8,128)} custom-call(f32[2,3,5,64,128]{4,3,2,1,0:T(8,128)} %donor_ref.1, f32[2,4,128]{2,1,0:T(4,128)} %weights_ref.1), custom_call_target="tpu_custom_call" | custom-call | tf_op jit(solution)/shard_map/pallas_call | solution.py:173
  2.1 0.0 copy-start.2
  2.1 16.4 %all-to-all-start = ((f32[128,15,1,128]{3,2,1,0:T(1,128)}), f32[128,15,1,128]{3,2,1,0:T(1,128)S(1)}, u32[]{:S(2)}, u32[]{:S(2)}) async-start(f32[128,15,1,128]{3,2,1,0:T(1,128)} %bitcast.7), calls=%async_computation | async-start | bytes 1966080 | tf_op jit(solution)/shard_map/all_to_all | solution.py:168
  18.5 0.0 copy-done.2
  18.5 0.0 copy-start
  18.5 0.0 copy-start.1
  18.5 0.6 copy-done
  19.2 0.0 copy-done.1
  19.2 1.5 %shard_map.56 = (f32[96,96]{1,0:T(8,128)S(1)}, s32[136]{0:T(256)S(1)}) custom-call(f32[2,17,17]{2,1,0:T(8,128)S(1)} %copy.9.time_shift_ref, s32[17]{0:T(128)S(1)} %copy-done.1, s32[2,4]{1,0:T(2,128)S(1)} %copy-done), custom_call_target="tpu_custom_call" | custom-call | tf_op jit(solution)/shard_map/pallas_call | solution.py:188
  20.7 29.6 %all-to-all-done = f32[128,15,1,128]{3,2,1,0:T(1,128)S(1)} async-done(((f32[128,15,1,128]{3,2,1,0:T(1,128)}), f32[128,15,1,128]{3,2,1,0:T(1,128)S(1)}, u32[]{:S(2)}, u32[]{:S(2)}) %all-to-all-start) | async-done | bytes 983072 | tf_op jit(solution)/shard_map/all_to_all | solution.py:168
  50.2 1.4 %shard_map.57 = f32[1920,128]{1,0:T(8,128)S(1)} custom-call(f32[1920,128]{1,0:T(8,128)S(1)} %bitcast.4, f32[96,96]{1,0:T(8,128)S(1)} %get-tuple-element.7.mix_ref, s32[136]{0:T(256)S(1)} %get-tuple-element.8.table_ref), custom_call_target="tpu_custom_call" | custom-call | tf_op jit(solution)/shard_map/pallas_call | solution.py:199
  51.6 33.6 %all_to_all.10 = f32[128,15,1,128]{3,2,1,0:T(1,128)S(1)} all-to-all(f32[128,15,1,128]{3,2,1,0:T(1,128)S(1)} %bitcast.5), channel_id=1, replica_groups=mesh['pitch'=16,'inst'=8,'span'=2] {'inst','pitch'}, dimensions={0} | all-to-all | bytes 1966080 | tf_op jit(solution)/shard_map/all_to_all | solution.py:168
  85.2 1.1 %shard_map.58 = f32[2,3,5,64,128]{4,3,2,1,0:T(8,128)} custom-call(f32[1920,128]{1,0:T(8,128)S(1)} %bitcast.6), custom_call_target="tpu_custom_call" | custom-call | tf_op jit(solution)/shard_map/pallas_call | solution.py:212
  (1 shorter events, 0.0 us)
Async XLA Ops:
  2.1 16.4 %copy-start.2 = (f32[2,17,17]{2,0,1:T(2,128)S(1)}, f32[2,17,17]{2,0,1:T(2,128)}, u32[]{:S(2)}) copy-start(f32[2,17,17]{2,0,1:T(2,128)} %param.6) | copy-start | bytes 6940
  2.1 48.2 %all-to-all-start = ((f32[128,15,1,128]{3,2,1,0:T(1,128)}), f32[128,15,1,128]{3,2,1,0:T(1,128)S(1)}, u32[]{:S(2)}, u32[]{:S(2)}) async-start(f32[128,15,1,128]{3,2,1,0:T(1,128)} %bitcast.7), calls=%async_computation | async-start | bytes 1966080 | tf_op jit(solution)/shard_map/all_to_all | solution.py:168
  18.5 0.7 copy-start
  18.5 0.7 copy-start.1

commit v7 on v6

--- a/solution.py
+++ b/solution.py
@@ -139,15 +139,22 @@
             sent_ref[place(m, v), :] = none
 
 
-def unpack_kernel(blocks, owners, got_ref, received_ref):
+def unpack_kernel(blocks, owners, got_ref, received_ref, held, sems):
     inst_dev, span = received_ref.shape[1], received_ref.shape[3]
     depth = inst_dev * VARS
-    first = pl.program_id(0) * (span // owners)
-    for c in range(span // owners):
-        for k in range(inst_dev):
-            for v in range(VARS):
-                rows = pl.ds((first + c) * depth + k * VARS + v, owners, stride=blocks * depth)
-                received_ref[0, k, v, c * owners : (c + 1) * owners] = got_ref[rows, :]
+    parts = [(r, k) for r in range(2) for k in range(inst_dev)]
+
+    def departure(r, k):
+        return pltpu.make_async_copy(held.at[r, k], received_ref.at[r, k], sems.at[r, k])
+
+    for r, k in parts:
+        for v in range(VARS):
+            for c in range(span // owners):
+                rows = pl.ds((r * (span // owners) + c) * depth + k * VARS + v, owners, stride=blocks * depth)
+                held[r, k, v, c * owners : (c + 1) * owners] = got_ref[rows, :]
+        departure(r, k).start()
+    for r, k in parts:
+        departure(r, k).wait()
 
 
 def my_row(peers, owners):
@@ -211,10 +218,10 @@
     back = exchanged(sent, ("inst", "pitch"))
     return pl.pallas_call(
         functools.partial(unpack_kernel, blocks, owners),
-        grid=(2,),
         out_shape=jax.ShapeDtypeStruct(donor_state.shape, jnp.float32),
         in_specs=[VMEM],
-        out_specs=pl.BlockSpec((1, inst_dev, VARS, span, lanes), lambda r: (r, 0, 0, 0, 0)),
+        out_specs=hbm,
+        scratch_shapes=[pltpu.VMEM(donor_state.shape, jnp.float32), pltpu.SemaphoreType.DMA((2, inst_dev))],
         compiler_params=params(8),
     )(back)
 

time: 86.9 us -> 86.9 us (level)
  no operation moved by 1% of the time
where the time goes in v7:
time: 86.9 us; the launch traced here: 86.3 us
  blocking collectives  33.6 us (39%)
  waiting for transfers between devices  29.6 us (34%)
  starting transfers between devices  16.4 us (19%)
  Pallas kernels  5.91 us (7%)
    all_to_all x1, blocking collectives, exchanged(): lax.all_to_all(whole, axes, 0, 0, tiled=True).reshape(peers * depth, lanes)  33.6 us
    all_to_all x1, waiting for transfers between devices, exchanged(): lax.all_to_all(whole, axes, 0, 0, tiled=True).reshape(peers * depth, lanes)  29.6 us
    all_to_all x1, starting transfers between devices, exchanged(): lax.all_to_all(whole, axes, 0, 0, tiled=True).reshape(peers * depth, lanes)  16.4 us
    pallas_call x1, Pallas kernels, on_device(): pl.pallas_call(functools.partial(pack_kernel, count), out_shape=jax.Shape...  2.04 us
  transfers between devices with their start and end apart: 1, of which 1 were waited for; matrix products, arithmetic and copies ran while one was open for 0% of the time, Pallas kernels for 2%

profile of v7, /device:TPU:1, one launch (start us, length us, event | category | flops | bytes accessed | tf_op | source)
XLA Modules:
  0.0 86.3 jit_solution(4323691757413790511)
XLA Ops:
  0.0 2.0 %shard_map.55 = f32[1920,128]{1,0:T(8,128)} custom-call(f32[2,3,5,64,128]{4,3,2,1,0:T(8,128)} %donor_ref.1, f32[2,4,128]{2,1,0:T(4,128)} %weights_ref.1), custom_call_target="tpu_custom_call" | custom-call | tf_op jit(solution)/shard_map/pallas_call | solution.py:180
  2.1 0.0 copy-start.2
  2.1 16.4 %all-to-all-start = ((f32[128,15,1,128]{3,2,1,0:T(1,128)}), f32[128,15,1,128]{3,2,1,0:T(1,128)S(1)}, u32[]{:S(2)}, u32[]{:S(2)}) async-start(f32[128,15,1,128]{3,2,1,0:T(1,128)} %bitcast.7), calls=%async_computation | async-start | bytes 1966080 | tf_op jit(solution)/shard_map/all_to_all | solution.py:175
  18.5 0.0 copy-done.2
  18.5 0.0 copy-start
  18.5 0.0 copy-start.1
  18.5 0.6 copy-done
  19.2 0.0 copy-done.1
  19.2 1.5 %shard_map.56 = (f32[96,96]{1,0:T(8,128)S(1)}, s32[136]{0:T(256)S(1)}) custom-call(f32[2,17,17]{2,1,0:T(8,128)S(1)} %copy.9.time_shift_ref, s32[17]{0:T(128)S(1)} %copy-done.1, s32[2,4]{1,0:T(2,128)S(1)} %copy-done), custom_call_target="tpu_custom_call" | custom-call | tf_op jit(solution)/shard_map/pallas_call | solution.py:195
  20.7 29.6 %all-to-all-done = f32[128,15,1,128]{3,2,1,0:T(1,128)S(1)} async-done(((f32[128,15,1,128]{3,2,1,0:T(1,128)}), f32[128,15,1,128]{3,2,1,0:T(1,128)S(1)}, u32[]{:S(2)}, u32[]{:S(2)}) %all-to-all-start) | async-done | bytes 983072 | tf_op jit(solution)/shard_map/all_to_all | solution.py:175
  50.2 1.4 %shard_map.57 = f32[1920,128]{1,0:T(8,128)S(1)} custom-call(f32[1920,128]{1,0:T(8,128)S(1)} %bitcast.4, f32[96,96]{1,0:T(8,128)S(1)} %get-tuple-element.7.mix_ref, s32[136]{0:T(256)S(1)} %get-tuple-element.8.table_ref), custom_call_target="tpu_custom_call" | custom-call | tf_op jit(solution)/shard_map/pallas_call | solution.py:206
  51.6 33.6 %all_to_all.10 = f32[128,15,1,128]{3,2,1,0:T(1,128)S(1)} all-to-all(f32[128,15,1,128]{3,2,1,0:T(1,128)S(1)} %bitcast.5), channel_id=1, replica_groups=mesh['pitch'=16,'inst'=8,'span'=2] {'inst','pitch'}, dimensions={0} | all-to-all | bytes 1966080 | tf_op jit(solution)/shard_map/all_to_all | solution.py:175
  85.2 1.0 %shard_map.58 = f32[2,3,5,64,128]{4,3,2,1,0:T(8,128)} custom-call(f32[1920,128]{1,0:T(8,128)S(1)} %bitcast.6), custom_call_target="tpu_custom_call" | custom-call | tf_op jit(solution)/shard_map/pallas_call | solution.py:219
  (1 shorter events, 0.0 us)
Async XLA Ops:
  2.1 16.4 %copy-start.2 = (f32[2,17,17]{2,0,1:T(2,128)S(1)}, f32[2,17,17]{2,0,1:T(2,128)}, u32[]{:S(2)}) copy-start(f32[2,17,17]{2,0,1:T(2,128)} %param.6) | copy-start | bytes 6940
  2.1 48.2 %all-to-all-start = ((f32[128,15,1,128]{3,2,1,0:T(1,128)}), f32[128,15,1,128]{3,2,1,0:T(1,128)S(1)}, u32[]{:S(2)}, u32[]{:S(2)}) async-start(f32[128,15,1,128]{3,2,1,0:T(1,128)} %bitcast.7), calls=%async_computation | async-start | bytes 1966080 | tf_op jit(solution)/shard_map/all_to_all | solution.py:175
  18.5 0.7 copy-start
  18.5 0.7 copy-start.1
